TPU v7x, 32 devices: a whole 2x2x4 slice. The times are simulated.
32 devices in a mesh: dp: 8 (over z, core), sp: 4 (over y, x).
Axes of the slice: x: 2, y: 2, z: 4, core: 2. Of those that a mesh axis runs over, the one named last changes fastest.
Arguments:
- tokens_in: bfloat16 [16, 1024, 1024], P('dp', 'sp'), may hold values from -6 to 6
- expert_ids: int32 [8, 4, 512, 1], P('dp', 'sp'), may hold values from 0 to 7; in each aligned block of 512 rows (0 to 511, 512 to 1023, ..., all dimensions but the last counted through in order) at most 128 rows name the same one
- query_weight: bfloat16 [1024, 1024], replicated, may hold values from -0.1875 to 0.1875
- key_weight: bfloat16 [1024, 1024], replicated, may hold values from -0.1875 to 0.1875
- value_weight: bfloat16 [1024, 1024], replicated, may hold values from -0.1875 to 0.1875
- out_weight: bfloat16 [1024, 1024], replicated, may hold values from -3 to 3
- norm1_gain: float32 [1024], replicated, may hold values from 0.25 to 1.75
- norm1_shift: float32 [1024], replicated, may hold values from -3 to 3
- norm2_gain: float32 [1024], replicated, may hold values from 0.25 to 1.75
- norm2_shift: float32 [1024], replicated, may hold values from -3 to 3
- up_weight: bfloat16 [8, 4096, 1024], P('dp'), may hold values from -0.1875 to 0.1875
- down_weight: bfloat16 [8, 4096, 1024], P('dp'), may hold values from -0.09375 to 0.09375
- out_cotangent: bfloat16 [16, 1024, 1024], P('dp', 'sp'), may hold values from -6 to 6
- load_mean: float32 [8], replicated, may hold values from 0.5 to 2
Outputs:
- block_out: bfloat16 [16, 1024, 1024], P('dp', 'sp')
- tokens_grad: bfloat16 [16, 1024, 1024], P('dp', 'sp')
- query_grad: float32 [1024, 1024], replicated
- key_grad: float32 [1024, 1024], replicated
- value_grad: float32 [1024, 1024], replicated
- out_grad: float32 [1024, 1024], replicated
- norm1_gain_grad: float32 [1024], replicated
- norm1_shift_grad: float32 [1024], replicated
- norm2_gain_grad: float32 [1024], replicated
- norm2_shift_grad: float32 [1024], replicated
- up_grad: float32 [8, 4096, 1024], P('dp', 'sp')
- down_grad: float32 [8, 4096, 1024], P('dp', 'sp')
- load_next: float32 [8], replicated
Inputs may be any that keep to these rules, and one draw needn't show every extreme that they name: `expert_ids`: among the 512 rows of one device no expert is named more than 128 times, and in some device's rows one expert is named exactly 128 times.
All inputs are finite; a program needn't handle non-finite values.
Results may differ from a plain program's by a relative error of at most 0.012.
Values may be sent and summed in bfloat16 or wider, within the bound.
A program may use at most 384 MiB of HBM per device.

v0:
```python
import functools

import jax
import jax.numpy as jnp
from jax import lax
from jax.experimental import pallas as pl
from jax.experimental.pallas import tpu as pltpu
from jax.sharding import PartitionSpec as P

HEADS = 16
MESH = pl.DeviceIdType.MESH
BLOCK = 256
LANES = 128
STEP = 1024
VMEM_BYTES = 60 * 2**20

NORM_EPSILON = 1e-05
GELU_ROOT = 0.7978845608028654
CUBIC_TERM = 0.044715

ROWS_BY_COLS = (((1,), (0,)), ((), ()))
ROWS_BY_ROWS = (((1,), (1,)), ((), ()))
COLS_BY_COLS = (((0,), (0,)), ((), ()))


def smooth(values):
    return (
        0.5
        * values
        * (1.0 + jnp.tanh(GELU_ROOT * (values + CUBIC_TERM * values * values * values)))
    )


def smooth_slope(values):
    inner = jnp.tanh(GELU_ROOT * (values + CUBIC_TERM * values * values * values))
    return 0.5 * (1.0 + inner) + 0.5 * values * (1.0 - inner * inner) * GELU_ROOT * (
        1.0 + 3.0 * CUBIC_TERM * values * values
    )


def norm_forward(values, gain, shift):
    center = jnp.mean(values, axis=-1, keepdims=True)
    offset = values - center
    rstd = lax.rsqrt(jnp.mean(offset * offset, axis=-1, keepdims=True) + NORM_EPSILON)
    unit = offset * rstd
    return (unit * gain + shift, unit, rstd)


def norm_backward(grad, unit, rstd, gain):
    scaled = grad * gain
    inner = (
        scaled
        - jnp.mean(scaled, axis=-1, keepdims=True)
        - unit * jnp.mean(scaled * unit, axis=-1, keepdims=True)
    )
    return (inner * rstd, jnp.sum(grad * unit, axis=0), jnp.sum(grad, axis=0))


def mxu(left, right, dims=ROWS_BY_COLS):
    return lax.dot_general(left, right, dims, preferred_element_type=jnp.float32)


def span(index, size):
    return pl.ds(pl.multiple_of(index * size, size), size)


def greet(peers):
    barrier = pltpu.get_barrier_semaphore()
    for peer in peers:
        pl.semaphore_signal(barrier, inc=1, device_id=peer, device_id_type=MESH)
    pl.semaphore_wait(barrier, len(peers))


def send(source, target, send_sem, recv_sem, peer):
    return pltpu.make_async_remote_copy(
        src_ref=source,
        dst_ref=target,
        send_sem=send_sem,
        recv_sem=recv_sem,
        device_id=peer,
        device_id_type=MESH,
    )


def exchange(others, source, target, send_sem, recv_sem):
    me = lax.axis_index("dp")
    return [
        send(
            source.at[flip(me, d)],
            target.at[me],
            send_sem.at[d],
            recv_sem.at[d],
            {"dp": flip(me, d)},
        )
        for d in range(1, others)
    ]


def flip(index, bits):
    bit = 1
    while bit <= bits:
        if bits & bit:
            index = index + bit - 2 * bit * lax.rem(index // bit, 2)
        bit *= 2
    return index


def forward(
    ways,
    others,
    head_dim,
    x_ref,
    cot_ref,
    wq_ref,
    wk_ref,
    wv_ref,
    wo_ref,
    ids_ref,
    gain1_ref,
    shift1_ref,
    gain2_ref,
    shift2_ref,
    normed_ref,
    q_ref,
    k_ref,
    v_ref,
    mixed_ref,
    arrived_ref,
    placer_ref,
    residual_ref,
    log_ref,
    outgoing_ref,
    counts_ref,
    x_all,
    cot_v,
    cot_out,
    wq_v,
    wk_v,
    wv_v,
    wo_v,
    placer_v,
    normed_v,
    q_v,
    k_v,
    v_v,
    mixed_f,
    mixed_h,
    mixed_tok,
    log_s,
    residual_v,
    normed2,
    x_send,
    x_recv,
    m_send,
    m_recv,
    c_send,
    c_recv,
    load_sem,
    x_sem,
    store_sem,
    own_sem,
):
    seqs, seq_len, model = x_all.shape
    shard = seq_len // ways
    width = q_v.shape[2]
    heads = width // head_dim
    slots = cot_out.shape[1]
    me = lax.axis_index("sp")
    dp = lax.axis_index("dp")
    peer = [flip(me, d) for d in range(ways)]
    near = (1, 2) if ways == 4 else tuple(range(1, ways))
    far = tuple(range(1 + len(near), ways))
    barrier = pltpu.get_barrier_semaphore()
    neighbours = [{"sp": peer[d]} for d in range(1, ways)]
    neighbours += [{"dp": flip(dp, d)} for d in range(1, others)]
    for device in neighbours:
        pl.semaphore_signal(barrier, inc=1, device_id=device, device_id_type=MESH)
    own_columns = span(me, width)
    loads = [
        pltpu.make_async_copy(source, target, load_sem.at[i])
        for i, (source, target) in enumerate(
            (
                (cot_ref, cot_v),
                (wq_ref.at[:, own_columns], wq_v),
                (wk_ref.at[:, own_columns], wk_v),
                (wv_ref.at[:, own_columns], wv_v),
                (wo_ref, wo_v),
            )
        )
    ]
    own_x = [
        pltpu.make_async_copy(x_ref.at[s], x_all.at[s, span(me, shard)], x_sem.at[s])
        for s in range(seqs)
    ]
    for copy in own_x + loads:
        copy.start()

    def x_copy(s, d):
        return send(
            x_ref.at[s],
            x_all.at[s, span(me, shard)],
            x_send.at[s, d],
            x_recv.at[s, d],
            {"sp": peer[d]},
        )

    def x_relays(s):
        if not far:
            return []
        size = shard // 2
        pieces = [
            x_all.at[s, pl.ds(pl.multiple_of(peer[1] * shard, size), size)],
            x_all.at[s, pl.ds(pl.multiple_of(peer[2] * shard + size, size), size)],
        ]
        return [
            send(piece, piece, x_send.at[s, at], x_recv.at[s, at], {"sp": peer[to]})
            for piece, at, to in zip(pieces, (0, 3), (2, 1))
        ]

    def mixed_copy(s, d):
        return send(
            mixed_h.at[s, span(peer[d], shard)],
            mixed_tok.at[s, :, own_columns],
            m_send.at[s, d],
            m_recv.at[s, d],
            {"sp": peer[d]},
        )

    tokens = seqs * shard
    ids = ids_ref[...]
    named = lax.broadcasted_iota(jnp.int32, (LANES, tokens), 0) == ids
    named = jnp.where(named, 1.0, 0.0)
    upper = lax.broadcasted_iota(jnp.int32, (tokens, tokens), 0) <= lax.broadcasted_iota(
        jnp.int32, (tokens, tokens), 1
    )
    running = mxu(named.astype(jnp.bfloat16), jnp.where(upper, 1.0, 0.0).astype(jnp.bfloat16))
    slot = jnp.sum(named * (running - 1.0), axis=0, keepdims=True).astype(jnp.int32)
    places = lax.broadcasted_iota(jnp.int32, placer_v.shape, 0) == ids * slots + slot
    placer_v[...] = jnp.where(places, 1.0, 0.0).astype(jnp.bfloat16)
    ones = jnp.ones((8, tokens), jnp.float32)
    counts_ref[...] = mxu(ones, named, ROWS_BY_ROWS)
    pl.semaphore_wait(barrier, len(neighbours))
    for d in near:
        x_copy(0, d).start()
    loads[0].wait()
    cot_out[...] = (
        mxu(placer_v[...], cot_v[...]).astype(jnp.bfloat16).reshape(cot_out.shape)
    )
    background = exchange(others, cot_out, arrived_ref, c_send, c_recv)
    own_cot = pltpu.make_async_copy(cot_out.at[dp], arrived_ref.at[dp], own_sem)
    for copy in background + [own_cot]:
        copy.start()

    lane = lax.broadcasted_iota(jnp.int32, (1, width), 1) // head_dim
    log_lane = lax.broadcasted_iota(jnp.int32, (1, LANES), 1)
    visible = lax.broadcasted_iota(jnp.int32, (BLOCK, BLOCK), 1) <= lax.broadcasted_iota(
        jnp.int32, (BLOCK, BLOCK), 0
    )
    scale = head_dim ** (-0.5)
    outs = ((normed_v, normed_ref), (q_v, q_ref), (k_v, k_ref), (v_v, v_ref))
    stores = [
        [
            pltpu.make_async_copy(source.at[s], target.at[s], store_sem.at[s, i])
            for i, (source, target) in enumerate(outs)
        ]
        for s in range(seqs)
    ]

    def project(s, d):
        rows = span(peer[d], shard)
        values = x_all[s, rows, :].astype(jnp.float32)
        normed, _, _ = norm_forward(values, gain1_ref[...], shift1_ref[...])
        normed = normed.astype(jnp.bfloat16)
        normed_v[s, rows, :] = normed
        q_v[s, rows, :] = mxu(normed, wq_v[...]).astype(jnp.bfloat16)
        k_v[s, rows, :] = mxu(normed, wk_v[...]).astype(jnp.bfloat16)
        v_v[s, rows, :] = mxu(normed, wv_v[...]).astype(jnp.bfloat16)

    for s in range(seqs):
        own_x[s].wait()
        if s == 0:
            for copy in loads[1:4]:
                copy.wait()
        project(s, 0)
        for d in near:
            x_copy(s, d).wait_recv()
        for copy in x_relays(s):
            copy.start()
        for d in near:
            project(s, d)
        for copy in x_relays(s):
            copy.wait_recv()
        if s + 1 < seqs:
            for d in near:
                x_copy(s + 1, d).start()
        if s:
            for d in range(1, ways):
                mixed_copy(s - 1, d).start()
        for d in far:
            project(s, d)
        for copy in stores[s]:
            copy.start()
        mixed_f[...] = jnp.zeros_like(mixed_f)
        log_s[...] = jnp.zeros_like(log_s)

        def one_head(h, carry):
            mine = (lane == h).astype(jnp.float32)
            for at in range(0, seq_len, BLOCK):
                rows = slice(at, at + BLOCK)
                query = (q_v[s, rows, :].astype(jnp.float32) * (mine * scale)).astype(
                    jnp.bfloat16
                )
                near = mxu(query, k_v[s, rows, :], ROWS_BY_ROWS)
                near = jnp.where(visible, near, -1e30)
                top = jnp.max(near, axis=1, keepdims=True)
                if at:
                    far = mxu(query, k_v[s, :at, :], ROWS_BY_ROWS)
                    top = jnp.maximum(top, jnp.max(far, axis=1, keepdims=True))
                near = jnp.exp(near - top)
                total = jnp.sum(near, axis=1, keepdims=True)
                if at:
                    far = jnp.exp(far - top)
                    total += jnp.sum(far, axis=1, keepdims=True)
                inverse = 1.0 / total
                out = mxu((near * inverse).astype(jnp.bfloat16), v_v[s, rows, :])
                if at:
                    out += mxu((far * inverse).astype(jnp.bfloat16), v_v[s, :at, :])
                mixed_f[rows, :] += out * mine
                log_s[rows, :] = jnp.where(log_lane == h, top + jnp.log(total), log_s[rows, :])
            return carry

        lax.fori_loop(0, heads, one_head, 0)
        log_ref[s] = jnp.transpose(log_s[...])[: log_ref.shape[1], :]
        mixed_h[s] = mixed_f[...].astype(jnp.bfloat16)
        mixed_tok[s, :, own_columns] = mixed_h[s, span(me, shard), :]
    for d in range(1, ways):
        mixed_copy(seqs - 1, d).start()

    loads[4].wait()
    for s in range(seqs):
        for d in range(1, ways):
            mixed_copy(s, d).wait_recv()
        rows = slice(s * shard, (s + 1) * shard)
        values = x_all[s, span(me, shard), :].astype(jnp.float32)
        values += mxu(mixed_tok[s], wo_v[...])
        residual_v[rows, :] = values
        normed, _, _ = norm_forward(values, gain2_ref[...], shift2_ref[...])
        normed2[rows, :] = normed.astype(jnp.bfloat16)
    last = [
        pltpu.make_async_copy(source, target, store_sem.at[seqs, i])
        for i, (source, target) in enumerate(
            ((mixed_tok, mixed_ref), (residual_v, residual_ref), (placer_v, placer_ref))
        )
    ]
    for copy in last:
        copy.start()
    outgoing_ref[...] = (
        mxu(placer_v[...], normed2[...]).astype(jnp.bfloat16).reshape(outgoing_ref.shape)
    )
    for s in range(seqs):
        for d in near:
            x_copy(s, d).wait_send()
        for copy in x_relays(s):
            copy.wait_send()
        for d in range(1, ways):
            mixed_copy(s, d).wait_send()
        for copy in stores[s]:
            copy.wait()
    for copy in background + [own_cot] + last:
        copy.wait()


def pair_of(sp):
    core = lax.rem(lax.axis_index("dp"), 2)
    along_x, along_y = flip(sp, 1), flip(sp, 2)
    return along_x + core * (along_y - along_x)


def shards_of(sp, ways):
    shards = [sp, flip(pair_of(sp), 3)]
    bit = 4
    while bit < ways:
        shards += [flip(shard, bit) for shard in shards]
        bit *= 2
    return shards


def run_experts(
    others,
    ways,
    outgoing_ref,
    cot_ref,
    up_ref,
    down_ref,
    back_ref,
    result_ref,
    up_own,
    up_rest,
    down_own,
    down_rest,
    received,
    arrived,
    up_v,
    down_v,
    hidden,
    slope_v,
    total,
    dn_own,
    dn_pair,
    dn_land,
    dnormed,
    out_pair,
    out_land,
    w_sem,
    o_sem,
    c_sem,
    a_send,
    a_recv,
    b_send,
    b_recv,
    f_send,
    f_recv,
    p_send,
    p_recv,
    e_send,
    e_recv,
):
    slots, width = received.shape[1:]
    rows = others * slots
    ff = up_v.shape[0]
    groups = others // 2
    me = lax.axis_index("dp")
    sp = lax.axis_index("sp")
    chip = me // 2
    pair = {"sp": pair_of(sp)}
    shards = shards_of(sp, ways)
    size = ff // len(shards)
    loads = [
        pltpu.make_async_copy(
            source.at[span(shard, size)], target.at[i * size : (i + 1) * size], w_sem.at[j, i]
        )
        for j, (source, target) in enumerate(((down_ref, down_v), (up_ref, up_v)))
        for i, shard in enumerate(shards)
    ]
    own_cot = pltpu.make_async_copy(cot_ref, arrived.at[0], c_sem.at[0])
    own_rows = pltpu.make_async_copy(outgoing_ref.at[me], received.at[me], c_sem.at[1])
    own_back = pltpu.make_async_copy(dnormed.at[me], back_ref.at[me], c_sem.at[2])
    own_rows.start()
    own_cot.start()
    for copy in loads:
        copy.start()
    greet([{"dp": flip(me, d)} for d in range(1, others)] + [pair])
    inward = exchange(others, outgoing_ref, received.at[0:others], a_send, a_recv)
    outward = exchange(others, dnormed, back_ref, b_send, b_recv)
    near = [flip(chip, group) for group in range(groups)]
    chips = [pl.ds(2 * near[group], 2) for group in range(groups)]
    forward = [
        send(
            received.at[chips[group]],
            received.at[pl.ds(others + 2 * near[group], 2)],
            f_send.at[group],
            f_recv.at[group],
            pair,
        )
        for group in range(groups)
    ]
    cot_copy = send(cot_ref, arrived.at[1], f_send.at[groups], f_recv.at[groups], pair)
    dn_copy = [
        send(
            dn_pair.at[chips[group]],
            dn_land.at[chips[group]],
            p_send.at[group],
            p_recv.at[group],
            pair,
        )
        for group in range(groups)
    ]
    out_copy = [
        send(
            out_pair.at[chips[group]],
            out_land.at[chips[group]],
            e_send.at[group],
            e_recv.at[group],
            pair,
        )
        for group in range(groups)
    ]

    early = range(groups // 2)
    middle = range(groups // 2, 3 * groups // 4)
    late = range(3 * groups // 4, groups)
    for copy in inward[: 2 * late[0] - 1]:
        copy.start()
    cot_copy.start()
    own_rows.wait()

    def slab_of(half, group):
        return pl.ds(pl.multiple_of(half * rows + near[group] * (2 * slots), 2 * slots), 2 * slots)

    def cot_half(half):
        def cot_step(i, carry):
            at = span(i, STEP)
            cot = arrived[half].reshape(rows, width)
            slope_v[half * rows : (half + 1) * rows, at] = mxu(
                cot, down_v[at, :], ROWS_BY_ROWS
            ).astype(jnp.bfloat16)
            return carry

        lax.fori_loop(0, ff // STEP, cot_step, 0)

    def up_half(half, group):
        slab = slab_of(half, group)
        total[...] = jnp.zeros_like(total)

        def up_step(i, carry):
            at = span(i, STEP)
            tokens = received[pl.ds(half * others + 2 * near[group], 2)].reshape(2 * slots, width)
            pre = mxu(tokens, up_v[at, :], ROWS_BY_ROWS)
            square = pre * pre
            inner = jnp.tanh(GELU_ROOT * pre * (1.0 + CUBIC_TERM * square))
            gate = 0.5 * (1.0 + inner)
            hidden[slab, at] = (pre * gate).astype(jnp.bfloat16)
            slope = gate + (0.5 * GELU_ROOT) * pre * (1.0 - inner * inner) * (
                1.0 + (3.0 * CUBIC_TERM) * square
            )
            dpre = (slope_v[slab, at].astype(jnp.float32) * slope).astype(jnp.bfloat16)
            slope_v[slab, at] = dpre
            total[...] += mxu(dpre, up_v[at, :])
            return carry

        lax.fori_loop(0, ff // STEP, up_step, 0)
        shaped = total[...].reshape(2, slots, width)
        if half:
            dn_pair[chips[group]] = shaped.astype(jnp.bfloat16)
            dn_copy[group].start()
        else:
            dn_own[chips[group]] = shaped

    def out_half(half, group):
        at = chips[group]
        out = mxu(hidden[slab_of(half, group), :], down_v[...]).reshape(2, slots, width)
        if half:
            out_pair[at] = out.astype(jnp.bfloat16)
            out_copy[group].start()
        else:
            out_copy[group].wait_recv()
            result_ref[at] = (out + out_land[at].astype(jnp.float32)).astype(jnp.bfloat16)

    def pass_on(group):
        for d in (2 * group, 2 * group + 1):
            if d:
                inward[d - 1].wait_recv()
        forward[group].start()

    def finish(group):
        dn_copy[group].wait_recv()
        at = chips[group]
        dnormed[at] = (dn_own[at] + dn_land[at].astype(jnp.float32)).astype(jnp.bfloat16)
        for d in (2 * group, 2 * group + 1):
            if d:
                outward[d - 1].start()
            else:
                own_back.start()

    def up_pair(group):
        forward[group].wait_recv()
        up_half(1, group)

    pass_on(0)
    own_cot.wait()
    for copy in loads[: len(shards)]:
        copy.wait()
    cot_half(0)
    for copy in loads[len(shards) :]:
        copy.wait()
    up_half(0, 0)
    for group in early[1:]:
        pass_on(group)
    for copy in inward[2 * middle[0] - 1 : 2 * late[0] - 1]:
        copy.wait_send()
    for copy in inward[2 * late[0] - 1 :]:
        copy.start()
    cot_copy.wait_recv()
    cot_half(1)
    for group in middle:
        pass_on(group)
    up_pair(0)
    for group in early[1:]:
        up_half(0, group)
        up_pair(group)
    for group in middle:
        up_half(0, group)
    for group in late:
        pass_on(group)
    for group in early:
        finish(group)
    for group in middle:
        up_pair(group)
    for group in late:
        up_half(0, group)
    for group in middle:
        finish(group)
    for group in late:
        up_pair(group)
    for group in range(groups):
        out_half(1, group)
    for group in late:
        finish(group)

    def grad(target, left, right_ref, block=0):
        def grad_step(i, carry):
            at = span(i, STEP)
            right = right_ref[...].reshape(2 * rows, width)
            out = mxu(left[:, at], right, COLS_BY_COLS).astype(jnp.bfloat16)
            if block:
                target[span(i, STEP // block)] = out.reshape(STEP // block, block, width)
            else:
                target[at, :] = out
            return carry

        lax.fori_loop(0, ff // STEP, grad_step, 0)

    grad(up_v, slope_v, received.at[0 : 2 * others])
    for copy in forward:
        copy.wait_send()
    grad(received, hidden, arrived, slots)
    first, every = size // slots, ff // slots
    stores = [
        pltpu.make_async_copy(source, target, o_sem.at[i])
        for i, (source, target) in enumerate(
            (
                (up_v.at[0:size], up_own),
                (up_v.at[size:ff], up_rest),
                (received.at[0:first], down_own),
                (received.at[first:every], down_rest),
            )
        )
    ]
    for copy in stores:
        copy.start()
    for group in range(groups):
        out_half(0, group)
    for copy in inward[: 2 * middle[0] - 1] + inward[2 * late[0] - 1 :]:
        copy.wait_send()
    for copy in [cot_copy] + dn_copy + out_copy:
        copy.wait_send()
    for copy in outward + stores + [own_back]:
        copy.wait()


class Reduction:
    def __init__(self, ways, columns, part, out, scratch):
        (
            self.core_land,
            self.core_sum,
            self.column_land,
            self.piece,
            core_send,
            core_recv,
            column_send,
            column_recv,
            spread_send,
            spread_recv,
            ring_send,
            ring_recv,
            cross_send,
            cross_recv,
            own_sem,
        ) = scratch
        me = lax.axis_index("sp")
        dp = lax.axis_index("dp")
        core = lax.rem(dp, 2)
        column = dp // 2
        twin = {"dp": dp + 1 - 2 * core}
        self.ways, self.columns, self.part = ways, columns, part
        self.core, self.column = core, column
        rows, width = self.piece.shape
        self.rows = rows

        def beside(d):
            return {"dp": 2 * lax.rem(column + d, columns) + core}

        def block(at_core, at_column, at_sp, count):
            first = pl.multiple_of((at_core * columns + at_column) * rows, rows)
            return out.at[pl.ds(first, count * rows), span(at_sp, width)]

        self.core_copy = send(
            part.at[span(1 - core, columns * rows)], self.core_land, core_send, core_recv, twin
        )
        self.column_copy = [
            send(
                self.core_sum.at[span(lax.rem(column + d, columns), rows)],
                self.column_land.at[d - 1],
                column_send.at[d],
                column_recv.at[d],
                beside(d),
            )
            for d in range(1, columns)
        ]
        spot = block(core, column, me, 1)
        self.own = pltpu.make_async_copy(self.piece, spot, own_sem)
        self.spread_copy = [
            send(self.piece, spot, spread_send.at[d], spread_recv.at[d], beside(d))
            for d in range(1, columns)
        ]
        origin = [flip(me, d) for d in range(ways)]
        half = [block(core, 0, at, columns) for at in origin]
        self.relays = []
        direct = range(1, ways)
        if ways == 4:
            direct = (1, 2)
            count = columns * rows // 2
            for i, (d, to) in enumerate(((1, 2), (2, 1))):
                first = pl.multiple_of(core * columns * rows + i * count, count)
                piece = out.at[pl.ds(first, count), span(origin[d], width)]
                self.relays.append(
                    send(piece, piece, ring_send.at[i], ring_recv.at[i], {"sp": origin[to]})
                )
            ring_send, ring_recv = ring_send.at[1:ways], ring_recv.at[1:ways]
        self.ring_copy = [
            send(half[0], half[0], ring_send.at[d], ring_recv.at[d], {"sp": origin[d]})
            for d in direct
        ]
        self.cross_copy = [
            send(half[d], half[d], cross_send.at[d], cross_recv.at[d], twin) for d in range(ways)
        ]

    def add_core(self):
        self.core_copy.wait()
        self.core_sum[...] = (
            self.part[span(self.core, self.columns * self.rows), :].astype(jnp.float32)
            + self.core_land[...].astype(jnp.float32)
        ).astype(jnp.bfloat16)
        for copy in self.column_copy:
            copy.start()

    def add_column(self):
        total = self.core_sum[span(self.column, self.rows), :].astype(jnp.float32)
        for d, copy in enumerate(self.column_copy):
            copy.wait()
            total += self.column_land[d].astype(jnp.float32)
        return total

    def spread(self):
        self.own.start()
        for copy in self.spread_copy:
            copy.start()

    def ring(self):
        self.own.wait()
        for copy in self.spread_copy:
            copy.wait()
        for copy in self.ring_copy:
            copy.start()
        self.cross_copy[0].start()

    def relay(self):
        for ring, cross in zip(self.ring_copy, self.cross_copy[1:]):
            ring.wait_recv()
            cross.start()
        for relay in self.relays:
            relay.start()

    def cross(self):
        for relay in self.relays:
            relay.wait_recv()
        if self.relays:
            self.cross_copy[3].start()

    def finish(self):
        for copy in self.ring_copy + self.relays:
            copy.wait_send()
        for copy in self.cross_copy:
            copy.wait()


def backward(
    ways,
    others,
    head_dim,
    back_ref,
    placer_ref,
    cot_ref,
    residual_ref,
    wo_ref,
    mixed_ref,
    q_ref,
    k_ref,
    v_ref,
    normed_ref,
    wq_ref,
    wk_ref,
    wv_ref,
    x_ref,
    result_ref,
    up_rest,
    down_rest,
    log_ref,
    gain1_ref,
    gain2_ref,
    counts_ref,
    out_q,
    out_k,
    out_v,
    out_o,
    up_land,
    down_land,
    block_ref,
    tokens_ref,
    small_out,
    back_v,
    placer_v,
    cot_v,
    residual_v,
    wo_v,
    mixed_v,
    q_v,
    k_v,
    v_v,
    normed_v,
    wq_v,
    wk_v,
    wv_v,
    x_v,
    returned,
    dresid,
    dattn,
    dmixed,
    dmixed_h,
    dq_f,
    dk_f,
    dv_f,
    grads_h,
    grads_tok,
    part_o,
    parts_w,
    o_land,
    small_own,
    small_land,
    small_sum,
    m_send,
    m_recv,
    g_send,
    g_recv,
    c_send,
    c_recv,
    s_send,
    s_recv,
    o_send,
    o_recv,
    small_send,
    small_recv,
    load_sem,
    *scratch,
):
    seqs, shard, model = x_v.shape
    seq_len, width = q_v.shape[1:]
    heads = width // head_dim
    columns = others // 2
    me = lax.axis_index("sp")
    dp = lax.axis_index("dp")
    core = lax.rem(dp, 2)
    peer = [lax.rem(me + d, ways) for d in range(ways)]
    barrier = pltpu.get_barrier_semaphore()
    neighbours = [{"sp": peer[d]} for d in range(1, ways)]
    neighbours += [{"dp": flip(dp, d)} for d in range(1, others)]
    for device in neighbours:
        pl.semaphore_signal(barrier, inc=1, device_id=device, device_id_type=MESH)
    sources = (
        (back_ref, back_v),
        (placer_ref, placer_v),
        (residual_ref, residual_v),
        (cot_ref, cot_v),
        (wo_ref, wo_v),
        (mixed_ref, mixed_v),
        (q_ref, q_v),
        (k_ref, k_v),
        (v_ref, v_v),
        (normed_ref, normed_v),
        (wq_ref, wq_v),
        (wk_ref, wk_v),
        (wv_ref, wv_v),
        (x_ref, x_v),
        (result_ref.at[dp], returned.at[dp]),
    )
    loads = [
        pltpu.make_async_copy(source, target, load_sem.at[i])
        for i, (source, target) in enumerate(sources)
    ]
    for copy in loads:
        copy.start()

    def dmixed_copy(s, d):
        return send(
            dmixed.at[s, :, span(peer[d], width)],
            dmixed_h.at[s, span(me, shard)],
            m_send.at[s, d],
            m_recv.at[s, d],
            {"sp": peer[d]},
        )

    def grad_copy(s, d):
        return send(
            grads_h.at[s, span(peer[d], shard)],
            grads_tok.at[s, :, span(me, 3 * width)],
            g_send.at[s, d],
            g_recv.at[s, d],
            {"sp": peer[d]},
        )

    small_own[...] = jnp.zeros_like(small_own)
    small_own[4:5, 0:LANES] = counts_ref[0:1, :]
    for s in range(seqs):
        if s == 0:
            for copy in loads[:4]:
                copy.wait()
        rows = slice(s * shard, (s + 1) * shard)
        dnormed = mxu(placer_v[:, rows], back_v[...].reshape(-1, model), COLS_BY_COLS)
        gain = gain2_ref[...]
        _, unit, rstd = norm_forward(residual_v[rows, :], gain, jnp.zeros_like(gain))
        dinput, gain_grad, shift_grad = norm_backward(dnormed, unit, rstd, gain)
        total = cot_v[rows, :].astype(jnp.float32) + dinput
        dresid[s] = total
        dattn[rows, :] = total.astype(jnp.bfloat16)
        small_own[2:3, :] += gain_grad.reshape(1, model)
        small_own[3:4, :] += shift_grad.reshape(1, model)
        if s == 0:
            loads[4].wait()
        dmixed[s] = mxu(dattn[rows, :], wo_v[...], ROWS_BY_ROWS).astype(jnp.bfloat16)
        if s == 0:
            pl.semaphore_wait(barrier, len(neighbours))
        for d in range(1, ways):
            dmixed_copy(s, d).start()
    routed_back = exchange(others, result_ref, returned, c_send, c_recv)
    for copy in routed_back[: others // 2 - 1]:
        copy.start()
    shards = shards_of(me, ways)
    scatter = []
    for j, (rest, land) in enumerate(((up_rest, up_land), (down_rest, down_land))):
        size = land.shape[1]
        scatter += [
            send(
                rest.at[(i - 1) * size : i * size],
                land.at[i - 1],
                s_send.at[j, i],
                s_recv.at[j, i],
                {"sp": shards[i]},
            )
            for i in range(1, len(shards))
        ]
    sum_o = Reduction(ways, columns, part_o, out_o, scratch[:15])
    sums_w = [
        Reduction(ways, columns, parts_w.at[i], out, scratch[15 * (i + 1) : 15 * (i + 2)])
        for i, out in enumerate((out_q, out_k, out_v))
    ]
    sum_q, sum_k, sum_v = sums_w

    loads[5].wait()

    def out_step(i, carry):
        at = span(i, BLOCK)
        left = mixed_v[:, :, at].reshape(seqs * shard, BLOCK)
        part_o[at, :] = mxu(left, dattn[...], COLS_BY_COLS).astype(jnp.bfloat16)
        return carry

    lax.fori_loop(0, model // BLOCK, out_step, 0)
    sum_o.core_copy.start()
    for copy in loads[6:9]:
        copy.wait()

    lane = lax.broadcasted_iota(jnp.int32, (1, width), 1) // head_dim
    visible = lax.broadcasted_iota(jnp.int32, (BLOCK, BLOCK), 0) <= lax.broadcasted_iota(
        jnp.int32, (BLOCK, BLOCK), 1
    )
    scale = head_dim ** (-0.5)
    for s in range(seqs):
        dmixed_h[s, span(me, shard), :] = dmixed[s, :, span(me, width)]
        for d in range(1, ways):
            dmixed_copy(s, d).wait_recv()
        if s == 0:
            sum_o.add_core()
            for copy in scatter:
                copy.start()
        dq_f[...] = jnp.zeros_like(dq_f)
        dk_f[...] = jnp.zeros_like(dk_f)
        dv_f[...] = jnp.zeros_like(dv_f)

        def one_head(h, carry):
            mine = (lane == h).astype(jnp.float32)
            for at in range(0, seq_len, BLOCK):
                rows = slice(at, at + BLOCK)
                query = (q_v[s, rows, :].astype(jnp.float32) * (mine * scale)).astype(
                    jnp.bfloat16
                )
                dout = (dmixed_h[s, rows, :].astype(jnp.float32) * mine).astype(jnp.bfloat16)
                log_row = log_ref[s, pl.ds(h, 1), rows]
                parts = [(rows, True)] + ([(slice(0, at), False)] if at else [])
                kept = []
                delta = jnp.zeros((1, BLOCK), jnp.float32)
                for keys, diagonal in parts:
                    prob = jnp.exp(mxu(k_v[s, keys, :], query, ROWS_BY_ROWS) - log_row)
                    if diagonal:
                        prob = jnp.where(visible, prob, 0.0)
                    dprob = mxu(v_v[s, keys, :], dout, ROWS_BY_ROWS)
                    delta += jnp.sum(prob * dprob, axis=0, keepdims=True)
                    kept.append((keys, prob, dprob))
                dquery = jnp.zeros((BLOCK, width), jnp.float32)
                for keys, prob, dprob in kept:
                    dv_f[keys, :] += mxu(prob.astype(jnp.bfloat16), dout)
                    dlogit = (prob * (dprob - delta)).astype(jnp.bfloat16)
                    dk_f[keys, :] += mxu(dlogit, query)
                    dquery += mxu(dlogit, k_v[s, keys, :], COLS_BY_COLS)
                dq_f[rows, :] += dquery * (mine * scale)
            return carry

        lax.fori_loop(0, heads, one_head, 0)
        for i, total in enumerate((dq_f, dk_f, dv_f)):
            grads_h[s, :, i * width : (i + 1) * width] = total[...].astype(jnp.bfloat16)
        for d in range(1, ways):
            grad_copy(s, d).start()
        grads_tok[s, :, span(me, 3 * width)] = grads_h[s, span(me, shard), :]
        if s == 0:
            for copy in routed_back[others // 2 - 1 : 3 * others // 4 - 1]:
                copy.start()

    loads[9].wait()

    def weight_step(i, carry):
        at = span(i, BLOCK)
        grad = mxu(normed_v[0, :, at], grads_h[0], COLS_BY_COLS)
        for s in range(1, seqs):
            grad += mxu(normed_v[s, :, at], grads_h[s], COLS_BY_COLS)
        for j in range(3):
            parts_w[j, at, :] = grad[:, j * width : (j + 1) * width].astype(jnp.bfloat16)
        return carry

    lax.fori_loop(0, model // BLOCK, weight_step, 0)
    for total in (sum_v, sum_k, sum_q):
        total.core_copy.start()

    o_land[0] = sum_o.add_column().astype(jnp.bfloat16)
    o_copy = [
        send(
            o_land.at[0, :, span(peer[d], width)],
            o_land.at[d, :, 0:width],
            o_send.at[d],
            o_recv.at[d],
            {"sp": peer[d]},
        )
        for d in range(1, ways)
    ]
    for copy in o_copy:
        copy.start()
    for total in (sum_v, sum_k, sum_q):
        total.add_core()
    for total in (sum_v, sum_k, sum_q):
        total.piece[...] = total.add_column().astype(jnp.bfloat16)
        total.spread()

    def norm_grad(s):
        for d in range(1, ways):
            grad_copy(s, d).wait()
        dnormed = jnp.zeros((shard, model), jnp.float32)
        for j in range(ways):
            for i, weight in enumerate((wq_v, wk_v, wv_v)):
                at = (3 * j + i) * width
                dnormed += mxu(
                    grads_tok[s, :, at : at + width],
                    weight[:, j * width : (j + 1) * width],
                    ROWS_BY_ROWS,
                )
        gain = gain1_ref[...]
        _, unit, rstd = norm_forward(x_v[s].astype(jnp.float32), gain, jnp.zeros_like(gain))
        dinput, gain_grad, shift_grad = norm_backward(dnormed, unit, rstd, gain)
        tokens_ref[s] = (dresid[s] + dinput).astype(jnp.bfloat16)
        small_own[0:1, :] += gain_grad.reshape(1, model)
        small_own[1:2, :] += shift_grad.reshape(1, model)

    for copy in loads[10:14]:
        copy.wait()
    for s in range(seqs - 1):
        norm_grad(s)
    sum_v.ring()
    total = o_land[0, :, span(me, width)].astype(jnp.float32)
    for d, copy in enumerate(o_copy):
        copy.wait()
        total += o_land[d + 1, :, 0:width].astype(jnp.float32)
    sum_o.piece[...] = total.astype(jnp.bfloat16)
    sum_o.spread()
    sum_k.ring()
    sum_q.ring()
    for copy in routed_back[3 * others // 4 - 1 :]:
        copy.start()
    sum_v.relay()
    norm_grad(seqs - 1)
    sum_o.ring()
    sum_k.relay()

    steps = [[{"dp": dp + 1 - 2 * core}]]
    steps.append([{"dp": 2 * lax.rem(dp // 2 + d, columns) + core} for d in range(1, columns)])
    steps.append([{"sp": peer[d]} for d in range(1, ways)])
    slot = 0
    source = small_own
    for number, peers in enumerate(steps):
        copies = [
            send(
                source,
                small_land.at[slot + i],
                small_send.at[slot + i],
                small_recv.at[slot + i],
                device,
            )
            for i, device in enumerate(peers)
        ]
        for copy in copies:
            copy.start()
        if number == 0:
            sum_q.relay()
        elif number == 1:
            sum_v.cross()
            sum_o.relay()
        total = source[...]
        for i, copy in enumerate(copies):
            copy.wait()
            total += small_land[slot + i]
        slot += len(peers)
        if number == len(steps) - 1:
            small_out[...] = total
        else:
            small_sum[number] = total
            source = small_sum.at[number]

    loads[14].wait()
    for copy in routed_back:
        copy.wait()
    for s in range(seqs):
        rows = slice(s * shard, (s + 1) * shard)
        out = mxu(placer_v[:, rows], returned[...].reshape(-1, model), COLS_BY_COLS)
        block_ref[s] = (residual_v[rows, :] + out).astype(jnp.bfloat16)
    sum_k.cross()
    sum_q.cross()
    sum_o.cross()
    for s in range(seqs):
        for d in range(1, ways):
            dmixed_copy(s, d).wait_send()
    for copy in scatter:
        copy.wait()
    for total in [sum_o] + sums_w:
        total.finish()


def vmem(count):
    return [pl.BlockSpec(memory_space=pltpu.VMEM)] * count


def params(collective_id):
    return pltpu.CompilerParams(
        collective_id=collective_id, has_side_effects=True, vmem_limit_bytes=VMEM_BYTES
    )


def dma(*shape):
    return pltpu.SemaphoreType.DMA(shape)


def local(
    tokens_in,
    expert_ids,
    query_weight,
    key_weight,
    value_weight,
    out_weight,
    norm1_gain,
    norm1_shift,
    norm2_gain,
    norm2_shift,
    up_weight,
    down_weight,
    out_cotangent,
    load_mean,
):
    seq_count, shard_len, model_width = tokens_in.shape
    row_count = seq_count * shard_len
    head_dim = model_width // HEADS
    dp_ways = lax.axis_size("dp")
    sp_ways = lax.axis_size("sp")
    sp_at = lax.axis_index("sp")
    seq_len = shard_len * sp_ways
    experts = load_mean.shape[0]
    slot_count = 2 * row_count // experts
    local_experts = up_weight.shape[0]
    ff_width = up_weight.shape[1]
    width = model_width // sp_ways
    bf16 = jnp.bfloat16
    f32 = jnp.float32

    def shape(*sizes, dtype=bf16):
        return jax.ShapeDtypeStruct(sizes, dtype)

    cot_b = out_cotangent.reshape(row_count, model_width)
    hbm = [pl.BlockSpec(memory_space=pl.ANY)]
    routed = shape(experts, slot_count, model_width)
    square = pltpu.VMEM((model_width, model_width), bf16)
    by_head = pltpu.VMEM((seq_count, seq_len, width), bf16)
    token_shape = (seq_count, shard_len, model_width)
    whole_tokens = pltpu.VMEM((seq_count, seq_len, model_width), bf16)
    weight_columns = pltpu.VMEM((model_width, width), bf16)
    slots = (experts * slot_count, row_count)
    flat = (row_count, model_width)
    (
        normed_all,
        query_h,
        key_h,
        value_h,
        mixed_b,
        arrived,
        placer,
        residual_stream,
        log_total,
        outgoing,
        counts,
    ) = pl.pallas_call(
        functools.partial(forward, sp_ways, dp_ways, head_dim),
        out_shape=[
            shape(seq_count, seq_len, model_width),
            shape(seq_count, seq_len, width),
            shape(seq_count, seq_len, width),
            shape(seq_count, seq_len, width),
            shape(*token_shape),
            routed,
            shape(*slots),
            shape(*flat, dtype=f32),
            shape(seq_count, 8, seq_len, dtype=f32),
            routed,
            shape(8, LANES, dtype=f32),
        ],
        in_specs=hbm * 6 + vmem(5),
        out_specs=hbm * 8 + vmem(3),
        scratch_shapes=[
            whole_tokens,
            pltpu.VMEM(flat, bf16),
            pltpu.VMEM(routed.shape, bf16),
            weight_columns,
            weight_columns,
            weight_columns,
            square,
            pltpu.VMEM(slots, bf16),
            whole_tokens,
            by_head,
            by_head,
            by_head,
            pltpu.VMEM((seq_len, width), f32),
            by_head,
            pltpu.VMEM(token_shape, bf16),
            pltpu.VMEM((seq_len, LANES), f32),
            pltpu.VMEM(flat, f32),
            pltpu.VMEM(flat, bf16),
            dma(seq_count, sp_ways),
            dma(seq_count, sp_ways),
            dma(seq_count, sp_ways),
            dma(seq_count, sp_ways),
            dma(dp_ways),
            dma(dp_ways),
            dma(5),
            dma(seq_count),
            dma(seq_count + 1, 4),
            pltpu.SemaphoreType.DMA,
        ],
        compiler_params=params(0),
    )(
        tokens_in,
        cot_b,
        query_weight,
        key_weight,
        value_weight,
        out_weight,
        expert_ids.reshape(1, row_count),
        *(
            vector.reshape(1, model_width)
            for vector in (norm1_gain, norm1_shift, norm2_gain, norm2_shift)
        ),
    )
    ff_own = ff_width // 2
    received_blocks = max(2 * experts, ff_own // slot_count)
    shard_size = ff_width // sp_ways
    rest = sp_ways // 2 - 1
    blocks = shard_size // slot_count
    dnormed_back, expert_out, up_own, up_rest, down_own, down_rest = pl.pallas_call(
        functools.partial(run_experts, dp_ways, sp_ways),
        out_shape=[
            routed,
            routed,
            shape(shard_size, model_width),
            shape(rest * shard_size, model_width),
            shape(blocks, slot_count, model_width),
            shape(rest * blocks, slot_count, model_width),
        ],
        in_specs=hbm * 4,
        out_specs=hbm + vmem(1) + hbm * 4,
        scratch_shapes=[
            pltpu.VMEM((received_blocks, slot_count, model_width), bf16),
            pltpu.VMEM((2,) + routed.shape, bf16),
            pltpu.VMEM((ff_own, model_width), bf16),
            pltpu.VMEM((ff_own, model_width), bf16),
            pltpu.VMEM((2 * experts * slot_count, ff_own), bf16),
            pltpu.VMEM((2 * experts * slot_count, ff_own), bf16),
            pltpu.VMEM((2 * slot_count, model_width), f32),
            pltpu.VMEM(routed.shape, f32),
            pltpu.VMEM(routed.shape, bf16),
            pltpu.VMEM(routed.shape, bf16),
            pltpu.VMEM(routed.shape, bf16),
            pltpu.VMEM(routed.shape, bf16),
            pltpu.VMEM(routed.shape, bf16),
            dma(2, sp_ways // 2),
            dma(4),
            dma(3),
            dma(dp_ways),
            dma(dp_ways),
            dma(dp_ways),
            dma(dp_ways),
            dma(dp_ways // 2 + 1),
            dma(dp_ways // 2 + 1),
            dma(dp_ways // 2 + 1),
            dma(dp_ways // 2 + 1),
            dma(dp_ways // 2),
            dma(dp_ways // 2),
        ],
        compiler_params=params(3),
    )(outgoing, arrived, up_weight[0], down_weight[0])
    columns = dp_ways // 2
    rows = model_width // dp_ways

    def reduction(part_width):
        return [
            pltpu.VMEM((columns * rows, part_width), bf16),
            pltpu.VMEM((columns * rows, part_width), bf16),
            pltpu.VMEM((columns - 1, rows, part_width), bf16),
            pltpu.VMEM((rows, width), bf16),
            pltpu.SemaphoreType.DMA,
            pltpu.SemaphoreType.DMA,
            dma(columns),
            dma(columns),
            dma(columns),
            dma(columns),
            dma(sp_ways),
            dma(sp_ways),
            dma(sp_ways),
            dma(sp_ways),
            pltpu.SemaphoreType.DMA,
        ]

    small_slots = 1 + (columns - 1) + (sp_ways - 1)
    whole = shape(model_width, model_width)
    tokens = pltpu.VMEM(token_shape, bf16)
    *weight_grads, up_land, down_land, block_out, tokens_grad, small_sum = pl.pallas_call(
        functools.partial(backward, sp_ways, dp_ways, head_dim),
        out_shape=[whole] * 4
        + [
            shape(rest, shard_size, model_width),
            shape(rest, blocks, slot_count, model_width),
            shape(*token_shape),
            shape(*token_shape),
            shape(8, model_width, dtype=f32),
        ],
        in_specs=hbm * 17 + vmem(4),
        out_specs=hbm * 6 + vmem(3),
        scratch_shapes=[
            pltpu.VMEM(routed.shape, bf16),
            pltpu.VMEM(placer.shape, bf16),
            pltpu.VMEM(flat, bf16),
            pltpu.VMEM(flat, f32),
            square,
            tokens,
            by_head,
            by_head,
            by_head,
            whole_tokens,
            square,
            square,
            square,
            tokens,
            pltpu.VMEM(routed.shape, bf16),
            pltpu.VMEM(token_shape, f32),
            pltpu.VMEM(flat, bf16),
            tokens,
            by_head,
            pltpu.VMEM((seq_len, width), f32),
            pltpu.VMEM((seq_len, width), f32),
            pltpu.VMEM((seq_len, width), f32),
            pltpu.VMEM((seq_count, seq_len, 3 * width), bf16),
            pltpu.VMEM((seq_count, shard_len, 3 * model_width), bf16),
            square,
            pltpu.VMEM((3, model_width, width), bf16),
            pltpu.VMEM((sp_ways, rows, model_width), bf16),
            pltpu.VMEM((8, model_width), f32),
            pltpu.VMEM((small_slots, 8, model_width), f32),
            pltpu.VMEM((2, 8, model_width), f32),
            dma(seq_count, sp_ways),
            dma(seq_count, sp_ways),
            dma(seq_count, sp_ways),
            dma(seq_count, sp_ways),
            dma(dp_ways),
            dma(dp_ways),
            dma(2, sp_ways // 2),
            dma(2, sp_ways // 2),
            dma(sp_ways),
            dma(sp_ways),
            dma(small_slots),
            dma(small_slots),
            dma(15),
        ]
        + reduction(model_width)
        + reduction(width) * 3,
        compiler_params=params(1),
    )(
        dnormed_back,
        placer,
        cot_b,
        residual_stream,
        out_weight,
        mixed_b,
        query_h,
        key_h,
        value_h,
        normed_all,
        query_weight,
        key_weight,
        value_weight,
        tokens_in,
        expert_out,
        up_rest,
        down_rest,
        log_total,
        norm1_gain.reshape(1, model_width),
        norm2_gain.reshape(1, model_width),
        counts,
    )
    shard_shape = (shard_size, model_width)
    up_grad, down_grad = (
        sum((land[i].reshape(shard_shape).astype(f32) for i in range(rest)), own.astype(f32))[None]
        for own, land in ((up_own, up_land), (down_own.reshape(shard_shape), down_land))
    )
    query_grad, key_grad, value_grad, out_grad = (grad.astype(f32) for grad in weight_grads)
    load_now = small_sum[4, :experts] * experts / (row_count * dp_ways * sp_ways)
    load_next = 0.9 * load_mean + 0.1 * load_now
    return (
        block_out,
        tokens_grad,
        query_grad,
        key_grad,
        value_grad,
        out_grad,
        small_sum[0],
        small_sum[1],
        small_sum[2],
        small_sum[3],
        up_grad,
        down_grad,
        load_next,
    )


def solution(mesh):
    return jax.shard_map(
        local,
        mesh=mesh,
        in_specs=(
            P("dp", "sp", None),
            P("dp", "sp", None, None),
            P(),
            P(),
            P(),
            P(),
            P(),
            P(),
            P(),
            P(),
            P("dp", None, None),
            P("dp", None, None),
            P("dp", "sp", None),
            P(),
        ),
        out_specs=(
            P("dp", "sp", None),
            P("dp", "sp", None),
            P(),
            P(),
            P(),
            P(),
            P(),
            P(),
            P(),
            P(),
            P("dp", "sp", None),
            P("dp", "sp", None),
            P(),
        ),
        check_vma=False,
    )
```

profile of v0, /device:TPU:9, one launch (start us, length us, event | category | flops | bytes accessed | tf_op | source)
XLA Modules:
  0.0 347.4 jit_solution(14931759545184250804)
XLA Ops:
  0.6 60.4 %shard_map.237 = (bf16[2,1024,1024]{2,1,0:T(8,128)(2,1)}, bf16[2,1024,256]{2,1,0:T(8,128)(2,1)}, bf16[2,1024,256]{2,1,0:T(8,128)(2,1)}, bf16[2,1024,256]{2,1,0:T...) custom-call(bf16[2,256,1024]{2,1,0:T(8,128)(2,1)} %x_ref.3, ...), custom_call_target="tpu_custom_call" | custom-call | tf_op jit(solution)/shard_map/pallas_call | solution.py:1222
  61.1 118.8 %shard_map.238 = (bf16[8,128,1024]{2,1,0:T(8,128)(2,1)}, bf16[8,128,1024]{2,1,0:T(8,128)(2,1)}, bf16[1024,1024]{1,0:T(8,128)(2,1)}, bf16[1024,1024]{1,0:T(8,128)...) custom-call(bf16[8,128,1024]{2,1,0:T(8,128)(2,1)} %get-tuple-element.39.outgoing_ref, ...), custom_call_target="tpu_custom_call" | custom-call | tf_op jit(solution)/shard_map/pallas_call | solution.py:1288
  179.8 0.0 copy-start.9
  179.9 0.0 copy-start.5
  179.9 144.3 %shard_map.239 = (bf16[1024,1024]{1,0:T(8,128)(2,1)}, bf16[1024,1024]{1,0:T(8,128)(2,1)}, bf16[1024,1024]{1,0:T(8,128)(2,1)}, bf16[1024,1024]{1,0:T(8,128)(2,1)}...) custom-call(bf16[8,128,1024]{2,1,0:T(8,128)(2,1)} %get-tuple-element, ...), custom_call_target="tpu_custom_call" | custom-call | tf_op jit(solution)/shard_map/pallas_call | solution.py:1355
  324.2 0.0 copy-done.9
  324.2 1.2 bitcast_add_fusion
  325.4 1.5 fusion.1
  326.9 0.0 copy-done.5
  326.9 0.0 copy-start.6
  326.9 4.7 %fusion = f32[1,1024,1024]{2,1,0:T(8,128)} fusion(bf16[1024,1024]{1,0:T(8,128)(2,1)S(1)} %copy-done.5, bf16[1,1024,1024]{2,1,0:T(8,128)(2,1)} %get-tuple-element.62), kind=kLoop, calls=%fused_computation.2 | loop fusion | flops 3145728 | bytes 8388608 | tf_op jit(solution)/shard_map/broadcast_in_dim | solution.py:1440
  331.6 0.0 copy-done.4
  331.6 0.0 copy-done.6
  331.6 3.1 convert_add_fusion
  334.7 0.0 copy-done.3
  334.7 2.5 convert_element_type.47
  337.1 0.0 copy-done.2
  337.1 2.5 convert_element_type.48
  339.6 0.0 copy-done.1
  339.6 2.5 convert_element_type.49
  342.1 2.5 convert_element_type.50
  344.6 1.0 copy.29
  345.6 0.6 copy-done.7
  346.2 1.0 copy.30
  (9 shorter events, 0.0 us)
Async XLA Ops:
  179.8 144.3 %copy-start.9 = (f32[8]{0:T(128)S(1)}, f32[8]{0:T(128)}, u32[]{:S(2)}) copy-start(f32[8]{0:T(128)} %param.27) | copy-start | bytes 100
  179.9 147.0 %copy-start.5 = (bf16[1024,1024]{1,0:T(8,128)(2,1)S(1)}, bf16[1024,1024]{1,0:T(8,128)(2,1)}, u32[]{:S(2)}) copy-start(bf16[1024,1024]{1,0:T(8,128)(2,1)} %get-tuple-element.61) | copy-start | bytes 6291460
  326.9 4.7 %copy-start.4 = (bf16[8,128,1024]{2,1,0:T(8,128)(2,1)S(1)}, bf16[8,128,1024]{2,1,0:T(8,128)(2,1)}, u32[]{:S(2)}) copy-start(bf16[8,128,1024]{2,1,0:T(8,128)(2,1)} %get-tuple-element.63) | copy-start | bytes 6291460
  326.9 4.7 %copy-start.6 = (bf16[1,8,128,1024]{3,2,1,0:T(8,128)(2,1)S(1)}, bf16[1,8,128,1024]{3,2,1,0:T(8,128)(2,1)}, u32[]{:S(2)}) copy-start(bf16[1,8,128,1024]{3,2,1,0:T(8,128)(2,1)} %get-tuple-element.64) | copy-start | bytes 6291460
  331.6 3.1 copy-start.3
  334.7 2.5 copy-start.2
  337.1 2.5 copy-start.1
  339.6 2.5 copy-start
  342.1 2.5 copy-start.8
  344.6 1.6 copy-start.7
where the time goes:
time: 352 us; the launch traced here: 347 us
  Pallas kernels  323 us (92%)
  other arithmetic  18.9 us (5%)
  local copies, waits for them, and re-layouts  4.12 us (1%)
    pallas_call x1, Pallas kernels, local(): pl.pallas_call(functools.partial(backward, sp_ways, dp_ways, head_dim), o...  144 us
    pallas_call x1, Pallas kernels, local(): pl.pallas_call(functools.partial(run_experts, dp_ways, sp_ways), out_shap...  119 us
    pallas_call x1, Pallas kernels, local(): pl.pallas_call(functools.partial(forward, sp_ways, dp_ways, head_dim), ou...  60.4 us
    convert_element_type x4, other arithmetic, local(): grad.astype(f32)  9.91 us

commit v1 on v0

--- a/solution.py
+++ b/solution.py
@@ -489,7 +489,9 @@
     early = range(groups // 2)
     middle = range(groups // 2, 3 * groups // 4)
     late = range(3 * groups // 4, groups)
-    for copy in inward[: 2 * late[0] - 1]:
+    for copy in [inward[0]] + inward[2 * middle[0] - 1 : 2 * late[0] - 1]:
+        copy.start()
+    for copy in inward[1 : 2 * middle[0] - 1]:
         copy.start()
     cot_copy.start()
     own_rows.wait()
@@ -541,7 +543,6 @@
         out = mxu(hidden[slab_of(half, group), :], down_v[...]).reshape(2, slots, width)
         if half:
             out_pair[at] = out.astype(jnp.bfloat16)
-            out_copy[group].start()
         else:
             out_copy[group].wait_recv()
             result_ref[at] = (out + out_land[at].astype(jnp.float32)).astype(jnp.bfloat16)
@@ -574,38 +575,41 @@
     for copy in loads[len(shards) :]:
         copy.wait()
     up_half(0, 0)
-    for group in early[1:]:
+    for group in middle:
         pass_on(group)
+        up_half(0, group)
     for copy in inward[2 * middle[0] - 1 : 2 * late[0] - 1]:
         copy.wait_send()
     for copy in inward[2 * late[0] - 1 :]:
         copy.start()
+    for group in early[1:]:
+        pass_on(group)
     cot_copy.wait_recv()
     cot_half(1)
-    for group in middle:
-        pass_on(group)
-    up_pair(0)
     for group in early[1:]:
         up_half(0, group)
+    for group in middle:
         up_pair(group)
+    up_pair(0)
     for group in middle:
-        up_half(0, group)
+        finish(group)
     for group in late:
         pass_on(group)
-    for group in early:
-        finish(group)
-    for group in middle:
+    for group in early[1:]:
         up_pair(group)
     for group in late:
         up_half(0, group)
     for group in middle:
-        finish(group)
+        out_half(1, group)
+    finish(0)
     for group in late:
         up_pair(group)
-    for group in range(groups):
+    for group in [*early, *late]:
         out_half(1, group)
-    for group in late:
+    for group in [*early[1:], *late]:
         finish(group)
+    for copy in out_copy:
+        copy.start()
 
     def grad(target, left, right_ref, block=0):
         def grad_step(i, carry):
@@ -649,7 +653,7 @@
 
 
 class Reduction:
-    def __init__(self, ways, columns, part, out, scratch):
+    def __init__(self, ways, columns, part, out, across_first, scratch):
         (
             self.core_land,
             self.core_sum,
@@ -673,57 +677,132 @@
         column = dp // 2
         twin = {"dp": dp + 1 - 2 * core}
         self.ways, self.columns, self.part = ways, columns, part
-        self.core, self.column = core, column
+        self.core = core
         rows, width = self.piece.shape
         self.rows = rows
 
-        def beside(d):
-            return {"dp": 2 * lax.rem(column + d, columns) + core}
-
-        def block(at_core, at_column, at_sp, count):
-            first = pl.multiple_of((at_core * columns + at_column) * rows, rows)
+        bits = [1 << i for i in range(columns.bit_length() - 1)]
+        place = 0
+        for bit in bits:
+            place = 2 * place + lax.rem(column // bit, 2)
+        self.place = place
+
+        def beside(bit):
+            return {"dp": 2 * flip(column, bit) + core}
+
+        def block(first, at_sp, count):
+            first = pl.multiple_of((core * columns + first) * rows, rows)
             return out.at[pl.ds(first, count * rows), span(at_sp, width)]
 
         self.core_copy = send(
             part.at[span(1 - core, columns * rows)], self.core_land, core_send, core_recv, twin
         )
-        self.column_copy = [
-            send(
-                self.core_sum.at[span(lax.rem(column + d, columns), rows)],
-                self.column_land.at[d - 1],
-                column_send.at[d],
-                column_recv.at[d],
-                beside(d),
+        self.column_copy, self.kept, self.lands = [], [], []
+        first, count, used = 0, columns, 0
+        for i, bit in enumerate(bits):
+            count //= 2
+            mine = lax.rem(column // bit, 2)
+            size = count * rows
+            gone = pl.ds(pl.multiple_of((first + (1 - mine) * count) * rows, size), size)
+            first = first + mine * count
+            self.kept.append(pl.ds(pl.multiple_of(first * rows, size), size))
+            land = self.column_land.at[used : used + size]
+            used += size
+            self.lands.append(land)
+            self.column_copy.append(
+                send(self.core_sum.at[gone], land, column_send.at[i], column_recv.at[i], beside(bit))
             )
-            for d in range(1, columns)
+        spot = block(place, me, 1)
+        self.own = pltpu.make_async_copy(self.piece, spot, own_sem)
+        origin = [flip(me, d) for d in range(ways)]
+        across_count = 1 if across_first else columns
+        across_at = place if across_first else 0
+        near = (1, 2) if ways == 4 else tuple(range(1, ways))
+        held = [block(across_at, at, across_count) for at in origin]
+        self.ring_copy = [
+            send(held[0], held[0], ring_send.at[d], ring_recv.at[d], {"sp": origin[d]})
+            for d in near
         ]
-        spot = block(core, column, me, 1)
-        self.own = pltpu.make_async_copy(self.piece, spot, own_sem)
-        self.spread_copy = [
-            send(self.piece, spot, spread_send.at[d], spread_recv.at[d], beside(d))
-            for d in range(1, columns)
+        self.relays = []
+        if ways == 4:
+            count = across_count * rows // 2
+            first = (core * columns + across_at) * rows
+            for i, (d, to) in enumerate(((1, 2), (2, 1))):
+                at = pl.multiple_of(first + i * count, count)
+                half = out.at[pl.ds(at, count), span(origin[d], width)]
+                index = (0, 3)[i]
+                self.relays.append(
+                    send(
+                        half, half, ring_send.at[index], ring_recv.at[index], {"sp": origin[to]}
+                    )
+                )
+
+        def rows_of(first, count):
+            first = pl.multiple_of((core * columns + first) * rows, rows)
+            return out.at[pl.ds(first, count * rows)]
+
+        self.spread_copy, gathered = [], [rows_of(place, 1)]
+        for i, bit in enumerate(reversed(bits)):
+            count = 1 << i
+            at = place - lax.rem(place, count)
+            spot = rows_of(at, count) if across_first else block(at, me, count)
+            gathered.append(rows_of(flip(at, count), count))
+            self.spread_copy.append(
+                send(spot, spot, spread_send.at[i], spread_recv.at[i], beside(bit))
+            )
+        crossing = gathered if across_first else held
+        self.cross_copy = [
+            send(part, part, cross_send.at[i], cross_recv.at[i], twin)
+            for i, part in enumerate(crossing)
         ]
-        origin = [flip(me, d) for d in range(ways)]
-        half = [block(core, 0, at, columns) for at in origin]
-        self.relays = []
-        direct = range(1, ways)
-        if ways == 4:
-            direct = (1, 2)
-            count = columns * rows // 2
-            for i, (d, to) in enumerate(((1, 2), (2, 1))):
-                first = pl.multiple_of(core * columns * rows + i * count, count)
-                piece = out.at[pl.ds(first, count), span(origin[d], width)]
-                self.relays.append(
-                    send(piece, piece, ring_send.at[i], ring_recv.at[i], {"sp": origin[to]})
-                )
-            ring_send, ring_recv = ring_send.at[1:ways], ring_recv.at[1:ways]
-        self.ring_copy = [
-            send(half[0], half[0], ring_send.at[d], ring_recv.at[d], {"sp": origin[d]})
-            for d in direct
-        ]
-        self.cross_copy = [
-            send(half[d], half[d], cross_send.at[d], cross_recv.at[d], twin) for d in range(ways)
-        ]
+        self.phases = iter(self.across_then_along() if across_first else self.along_then_across())
+
+    def along_then_across(self):
+        self.own.start()
+        self.own.wait()
+        for copy in self.spread_copy:
+            copy.start()
+            yield
+            copy.wait()
+        for copy in self.ring_copy:
+            copy.start()
+        self.cross_copy[0].start()
+        yield
+        for ring, cross in zip(self.ring_copy, self.cross_copy[1:]):
+            ring.wait_recv()
+            cross.start()
+        for copy in self.relays:
+            copy.start()
+        yield
+        for copy in self.relays:
+            copy.wait_recv()
+        if self.relays:
+            self.cross_copy[3].start()
+        yield
+
+    def across_then_along(self):
+        self.own.start()
+        self.own.wait()
+        for copy in self.ring_copy:
+            copy.start()
+        yield
+        for copy in self.ring_copy:
+            copy.wait_recv()
+        for copy in self.relays:
+            copy.start()
+        yield
+        for copy in self.relays:
+            copy.wait_recv()
+        for spread, cross in zip(self.spread_copy, self.cross_copy):
+            spread.start()
+            cross.start()
+            yield
+            spread.wait()
+        self.cross_copy[-1].start()
+        yield
+
+    def advance(self):
+        next(self.phases)
 
     def add_core(self):
         self.core_copy.wait()
@@ -731,41 +810,16 @@
             self.part[span(self.core, self.columns * self.rows), :].astype(jnp.float32)
             + self.core_land[...].astype(jnp.float32)
         ).astype(jnp.bfloat16)
-        for copy in self.column_copy:
-            copy.start()
-
-    def add_column(self):
-        total = self.core_sum[span(self.column, self.rows), :].astype(jnp.float32)
-        for d, copy in enumerate(self.column_copy):
-            copy.wait()
-            total += self.column_land[d].astype(jnp.float32)
+        self.column_copy[0].start()
+
+    def add_column(self, step):
+        self.column_copy[step].wait()
+        total = self.core_sum[self.kept[step], :].astype(jnp.float32)
+        total += self.lands[step][...].astype(jnp.float32)
+        if step + 1 < len(self.column_copy):
+            self.core_sum[self.kept[step], :] = total.astype(jnp.bfloat16)
+            self.column_copy[step + 1].start()
         return total
-
-    def spread(self):
-        self.own.start()
-        for copy in self.spread_copy:
-            copy.start()
-
-    def ring(self):
-        self.own.wait()
-        for copy in self.spread_copy:
-            copy.wait()
-        for copy in self.ring_copy:
-            copy.start()
-        self.cross_copy[0].start()
-
-    def relay(self):
-        for ring, cross in zip(self.ring_copy, self.cross_copy[1:]):
-            ring.wait_recv()
-            cross.start()
-        for relay in self.relays:
-            relay.start()
-
-    def cross(self):
-        for relay in self.relays:
-            relay.wait_recv()
-        if self.relays:
-            self.cross_copy[3].start()
 
     def finish(self):
         for copy in self.ring_copy + self.relays:
@@ -908,6 +962,20 @@
             {"sp": peer[d]},
         )
 
+    shards = shards_of(me, ways)
+    scatter = []
+    for j, (rest, land) in enumerate(((up_rest, up_land), (down_rest, down_land))):
+        size = land.shape[1]
+        scatter += [
+            send(
+                rest.at[(i - 1) * size : i * size],
+                land.at[i - 1],
+                s_send.at[j, i],
+                s_recv.at[j, i],
+                {"sp": shards[i]},
+            )
+            for i in range(1, len(shards))
+        ]
     small_own[...] = jnp.zeros_like(small_own)
     small_own[4:5, 0:LANES] = counts_ref[0:1, :]
     for s in range(seqs):
@@ -931,29 +999,16 @@
             pl.semaphore_wait(barrier, len(neighbours))
         for d in range(1, ways):
             dmixed_copy(s, d).start()
+    for copy in scatter:
+        copy.start()
     routed_back = exchange(others, result_ref, returned, c_send, c_recv)
-    for copy in routed_back[: others // 2 - 1]:
-        copy.start()
-    shards = shards_of(me, ways)
-    scatter = []
-    for j, (rest, land) in enumerate(((up_rest, up_land), (down_rest, down_land))):
-        size = land.shape[1]
-        scatter += [
-            send(
-                rest.at[(i - 1) * size : i * size],
-                land.at[i - 1],
-                s_send.at[j, i],
-                s_recv.at[j, i],
-                {"sp": shards[i]},
-            )
-            for i in range(1, len(shards))
-        ]
-    sum_o = Reduction(ways, columns, part_o, out_o, scratch[:15])
+    sum_o = Reduction(ways, columns, part_o, out_o, False, scratch[:15])
     sums_w = [
-        Reduction(ways, columns, parts_w.at[i], out, scratch[15 * (i + 1) : 15 * (i + 2)])
+        Reduction(ways, columns, parts_w.at[i], out, False, scratch[15 * (i + 1) : 15 * (i + 2)])
         for i, out in enumerate((out_q, out_k, out_v))
     ]
     sum_q, sum_k, sum_v = sums_w
+    steps = columns.bit_length() - 1
 
     loads[5].wait()
 
@@ -979,8 +1034,6 @@
             dmixed_copy(s, d).wait_recv()
         if s == 0:
             sum_o.add_core()
-            for copy in scatter:
-                copy.start()
         dq_f[...] = jnp.zeros_like(dq_f)
         dk_f[...] = jnp.zeros_like(dk_f)
         dv_f[...] = jnp.zeros_like(dv_f)
@@ -1016,29 +1069,16 @@
         lax.fori_loop(0, heads, one_head, 0)
         for i, total in enumerate((dq_f, dk_f, dv_f)):
             grads_h[s, :, i * width : (i + 1) * width] = total[...].astype(jnp.bfloat16)
-        for d in range(1, ways):
-            grad_copy(s, d).start()
+        if s == 0:
+            for d in range(1, ways):
+                grad_copy(s, d).start()
+            for step in range(steps - 1):
+                sum_o.add_column(step)
+            for copy in routed_back[: 3 * others // 4 - 1]:
+                copy.start()
         grads_tok[s, :, span(me, 3 * width)] = grads_h[s, span(me, shard), :]
-        if s == 0:
-            for copy in routed_back[others // 2 - 1 : 3 * others // 4 - 1]:
-                copy.start()
-
-    loads[9].wait()
-
-    def weight_step(i, carry):
-        at = span(i, BLOCK)
-        grad = mxu(normed_v[0, :, at], grads_h[0], COLS_BY_COLS)
-        for s in range(1, seqs):
-            grad += mxu(normed_v[s, :, at], grads_h[s], COLS_BY_COLS)
-        for j in range(3):
-            parts_w[j, at, :] = grad[:, j * width : (j + 1) * width].astype(jnp.bfloat16)
-        return carry
-
-    lax.fori_loop(0, model // BLOCK, weight_step, 0)
-    for total in (sum_v, sum_k, sum_q):
-        total.core_copy.start()
-
-    o_land[0] = sum_o.add_column().astype(jnp.bfloat16)
+
+    o_land[0] = sum_o.add_column(steps - 1).astype(jnp.bfloat16)
     o_copy = [
         send(
             o_land.at[0, :, span(peer[d], width)],
@@ -1051,11 +1091,35 @@
     ]
     for copy in o_copy:
         copy.start()
+
+    loads[9].wait()
+
+    def weight_step(i, carry):
+        at = span(i, BLOCK)
+        grad = mxu(normed_v[0, :, at], grads_h[0], COLS_BY_COLS)
+        for s in range(1, seqs):
+            grad += mxu(normed_v[s, :, at], grads_h[s], COLS_BY_COLS)
+        for j in range(3):
+            parts_w[j, at, :] = grad[:, j * width : (j + 1) * width].astype(jnp.bfloat16)
+        return carry
+
+    lax.fori_loop(0, model // BLOCK, weight_step, 0)
+    for total in (sum_v, sum_k, sum_q):
+        total.core_copy.start()
+
     for total in (sum_v, sum_k, sum_q):
         total.add_core()
-    for total in (sum_v, sum_k, sum_q):
-        total.piece[...] = total.add_column().astype(jnp.bfloat16)
-        total.spread()
+    for step in range(steps):
+        for total in (sum_v, sum_k, sum_q):
+            piece = total.add_column(step)
+            if step == steps - 1:
+                total.piece[...] = piece.astype(jnp.bfloat16)
+                total.advance()
+    for s in range(1, seqs):
+        for d in range(1, ways):
+            grad_copy(s, d).start()
+    for copy in routed_back[3 * others // 4 - 1 :]:
+        copy.start()
 
     def norm_grad(s):
         for d in range(1, ways):
@@ -1078,30 +1142,28 @@
 
     for copy in loads[10:14]:
         copy.wait()
+    for _ in range(steps - 1):
+        for total in (sum_v, sum_k, sum_q):
+            total.advance()
     for s in range(seqs - 1):
         norm_grad(s)
-    sum_v.ring()
+    for total in (sum_v, sum_k, sum_q):
+        total.advance()
     total = o_land[0, :, span(me, width)].astype(jnp.float32)
     for d, copy in enumerate(o_copy):
         copy.wait()
         total += o_land[d + 1, :, 0:width].astype(jnp.float32)
     sum_o.piece[...] = total.astype(jnp.bfloat16)
-    sum_o.spread()
-    sum_k.ring()
-    sum_q.ring()
-    for copy in routed_back[3 * others // 4 - 1 :]:
-        copy.start()
-    sum_v.relay()
+    sum_o.advance()
     norm_grad(seqs - 1)
-    sum_o.ring()
-    sum_k.relay()
-
-    steps = [[{"dp": dp + 1 - 2 * core}]]
-    steps.append([{"dp": 2 * lax.rem(dp // 2 + d, columns) + core} for d in range(1, columns)])
-    steps.append([{"sp": peer[d]} for d in range(1, ways)])
+    for _ in range(steps):
+        sum_o.advance()
+
+    stages = [[{"sp": peer[d]} for d in range(1, ways)], [{"dp": dp + 1 - 2 * core}]]
+    stages.append([{"dp": 2 * lax.rem(dp // 2 + d, columns) + core} for d in range(1, columns)])
     slot = 0
     source = small_own
-    for number, peers in enumerate(steps):
+    for number, peers in enumerate(stages):
         copies = [
             send(
                 source,
@@ -1115,16 +1177,20 @@
         for copy in copies:
             copy.start()
         if number == 0:
-            sum_q.relay()
+            sum_v.advance()
+            sum_k.advance()
         elif number == 1:
-            sum_v.cross()
-            sum_o.relay()
+            sum_q.advance()
+            sum_o.advance()
+        else:
+            sum_v.advance()
+            sum_k.advance()
         total = source[...]
         for i, copy in enumerate(copies):
             copy.wait()
             total += small_land[slot + i]
         slot += len(peers)
-        if number == len(steps) - 1:
+        if number == len(stages) - 1:
             small_out[...] = total
         else:
             small_sum[number] = total
@@ -1137,9 +1203,8 @@
         rows = slice(s * shard, (s + 1) * shard)
         out = mxu(placer_v[:, rows], returned[...].reshape(-1, model), COLS_BY_COLS)
         block_ref[s] = (residual_v[rows, :] + out).astype(jnp.bfloat16)
-    sum_k.cross()
-    sum_q.cross()
-    sum_o.cross()
+    sum_q.advance()
+    sum_o.advance()
     for s in range(seqs):
         for d in range(1, ways):
             dmixed_copy(s, d).wait_send()
@@ -1147,6 +1212,55 @@
         copy.wait()
     for total in [sum_o] + sums_w:
         total.finish()
+
+
+def finish(
+    experts,
+    tokens,
+    query_ref,
+    key_ref,
+    value_ref,
+    out_ref,
+    up_own,
+    up_land,
+    down_own,
+    down_land,
+    block_in,
+    tokens_in,
+    small_ref,
+    load_ref,
+    query_out,
+    key_out,
+    value_out,
+    out_out,
+    up_out,
+    down_out,
+    block_out,
+    tokens_out,
+    gain1_out,
+    shift1_out,
+    gain2_out,
+    shift2_out,
+    load_out,
+):
+    for source, target in (
+        (query_ref, query_out),
+        (key_ref, key_out),
+        (value_ref, value_out),
+        (out_ref, out_out),
+    ):
+        target[...] = source[...].astype(jnp.float32)
+    for own, land, target in ((up_own, up_land, up_out), (down_own, down_land, down_out)):
+        total = own[...].astype(jnp.float32)
+        for i in range(land.shape[0]):
+            total += land[i].astype(jnp.float32)
+        target[...] = total
+    block_out[...] = block_in[...]
+    tokens_out[...] = tokens_in[...]
+    for i, target in enumerate((gain1_out, shift1_out, gain2_out, shift2_out)):
+        target[...] = small_ref[i : i + 1, :]
+    load_now = small_ref[4:5, 0:experts] * experts / tokens
+    load_out[...] = 0.9 * load_ref[...] + 0.1 * load_now
 
 
 def vmem(count):
@@ -1334,7 +1448,7 @@
         return [
             pltpu.VMEM((columns * rows, part_width), bf16),
             pltpu.VMEM((columns * rows, part_width), bf16),
-            pltpu.VMEM((columns - 1, rows, part_width), bf16),
+            pltpu.VMEM(((columns - 1) * rows, part_width), bf16),
             pltpu.VMEM((rows, width), bf16),
             pltpu.SemaphoreType.DMA,
             pltpu.SemaphoreType.DMA,
@@ -1436,27 +1550,45 @@
         counts,
     )
     shard_shape = (shard_size, model_width)
-    up_grad, down_grad = (
-        sum((land[i].reshape(shard_shape).astype(f32) for i in range(rest)), own.astype(f32))[None]
-        for own, land in ((up_own, up_land), (down_own.reshape(shard_shape), down_land))
+    parts = 8
+    big = pl.BlockSpec((model_width // parts, model_width), lambda i: (i, 0))
+    own = pl.BlockSpec((shard_size // parts, model_width), lambda i: (i, 0))
+    land = pl.BlockSpec((rest, shard_size // parts, model_width), lambda i: (0, i, 0))
+    token = pl.BlockSpec((row_count // parts, model_width), lambda i: (i, 0))
+    row = pl.BlockSpec((1, model_width), lambda i: (0, 0))
+    load = pl.BlockSpec((1, experts), lambda i: (0, 0))
+    results = pl.pallas_call(
+        functools.partial(finish, experts, row_count * dp_ways * sp_ways),
+        grid=(parts,),
+        out_shape=[shape(model_width, model_width, dtype=f32)] * 4
+        + [shape(*shard_shape, dtype=f32)] * 2
+        + [shape(*flat)] * 2
+        + [shape(1, model_width, dtype=f32)] * 4
+        + [shape(1, experts, dtype=f32)],
+        in_specs=[big] * 4
+        + [own, land, own, land, token, token]
+        + [pl.BlockSpec((8, model_width), lambda i: (0, 0)), load],
+        out_specs=[big] * 4 + [own, own, token, token] + [row] * 4 + [load],
+        compiler_params=pltpu.CompilerParams(vmem_limit_bytes=VMEM_BYTES),
+    )(
+        *weight_grads,
+        up_own,
+        up_land,
+        down_own.reshape(shard_shape),
+        down_land.reshape((rest,) + shard_shape),
+        block_out.reshape(flat),
+        tokens_grad.reshape(flat),
+        small_sum,
+        load_mean.reshape(1, experts),
     )
-    query_grad, key_grad, value_grad, out_grad = (grad.astype(f32) for grad in weight_grads)
-    load_now = small_sum[4, :experts] * experts / (row_count * dp_ways * sp_ways)
-    load_next = 0.9 * load_mean + 0.1 * load_now
     return (
-        block_out,
-        tokens_grad,
-        query_grad,
-        key_grad,
-        value_grad,
-        out_grad,
-        small_sum[0],
-        small_sum[1],
-        small_sum[2],
-        small_sum[3],
-        up_grad,
-        down_grad,
-        load_next,
+        results[6].reshape(token_shape),
+        results[7].reshape(token_shape),
+        *results[:4],
+        *(vector.reshape(model_width) for vector in results[8:12]),
+        results[4][None],
+        results[5][None],
+        results[12].reshape(experts),
     )
 
 

time: 352 us -> 328 us (0.932)
  the two profiles are of different devices: /device:TPU:9 before, /device:TPU:0 now
where the time goes in v1:
time: 328 us; the launch traced here: 324 us
  Pallas kernels  323 us (98%)
    pallas_call x1, Pallas kernels, local(): pl.pallas_call(functools.partial(backward, sp_ways, dp_ways, head_dim), o...  140 us
    pallas_call x1, Pallas kernels, local(): pl.pallas_call(functools.partial(run_experts, dp_ways, sp_ways), out_shap...  101 us
    pallas_call x1, Pallas kernels, local(): pl.pallas_call(functools.partial(forward, sp_ways, dp_ways, head_dim), ou...  65.8 us
    pallas_call x1, Pallas kernels, local(): pl.pallas_call(functools.partial(finish, experts, row_count * dp_ways * s...  16.5 us

profile of v1, /device:TPU:0, one launch (start us, length us, event | category | flops | bytes accessed | tf_op | source)
XLA Modules:
  0.0 323.7 jit_solution(4517267073410648016)
XLA Ops:
  0.6 65.8 %shard_map.237 = (bf16[2,1024,1024]{2,1,0:T(8,128)(2,1)}, bf16[2,1024,256]{2,1,0:T(8,128)(2,1)}, bf16[2,1024,256]{2,1,0:T(8,128)(2,1)}, bf16[2,1024,256]{2,1,0:T...) custom-call(bf16[2,256,1024]{2,1,0:T(8,128)(2,1)} %x_ref.3, ...), custom_call_target="tpu_custom_call" | custom-call | tf_op jit(solution)/shard_map/pallas_call | solution.py:1336
  66.5 100.7 %shard_map.238 = (bf16[8,128,1024]{2,1,0:T(8,128)(2,1)}, bf16[8,128,1024]{2,1,0:T(8,128)(2,1)}, bf16[1024,1024]{1,0:T(8,128)(2,1)}, bf16[1024,1024]{1,0:T(8,128)...) custom-call(bf16[8,128,1024]{2,1,0:T(8,128)(2,1)} %get-tuple-element.52.outgoing_ref, ...), custom_call_target="tpu_custom_call" | custom-call | tf_op jit(solution)/shard_map/pallas_call | solution.py:1402
  167.2 139.7 %shard_map.239 = (bf16[1024,1024]{1,0:T(8,128)(2,1)}, bf16[1024,1024]{1,0:T(8,128)(2,1)}, bf16[1024,1024]{1,0:T(8,128)(2,1)}, bf16[1024,1024]{1,0:T(8,128)(2,1)}...) custom-call(bf16[8,128,1024]{2,1,0:T(8,128)(2,1)} %get-tuple-element, ...), custom_call_target="tpu_custom_call" | custom-call | tf_op jit(solution)/shard_map/pallas_call | solution.py:1469
  307.0 16.5 %shard_map.240 = (f32[1024,1024]{1,0:T(8,128)}, f32[1024,1024]{1,0:T(8,128)}, f32[1024,1024]{1,0:T(8,128)}, f32[1024,1024]{1,0:T(8,128)}, f32[1024,1024]{1,0:T(8...) custom-call(bf16[1024,1024]{1,0:T(8,128)(2,1)} %get-tuple-element.67, ...), custom_call_target="tpu_custom_call" | custom-call | tf_op jit(solution)/shard_map/pallas_call | solution.py:1560

commit v2 on v1

--- a/solution.py
+++ b/solution.py
@@ -217,12 +217,16 @@
             for piece, at, to in zip(pieces, (0, 3), (2, 1))
         ]
 
-    def mixed_copy(s, d):
+    cuts = max(1, width // BLOCK)
+    cuts = 2 * cuts if width // (2 * cuts) % LANES == 0 else cuts
+    cut = width // cuts
+
+    def mixed_copy(s, d, c):
         return send(
-            mixed_h.at[s, span(peer[d], shard)],
-            mixed_tok.at[s, :, own_columns],
-            m_send.at[s, d],
-            m_recv.at[s, d],
+            mixed_h.at[s, span(peer[d], shard), c * cut : (c + 1) * cut],
+            mixed_tok.at[s, :, span(me * cuts + c, cut)],
+            m_send.at[s, c, d],
+            m_recv.at[s, c, d],
             {"sp": peer[d]},
         )
 
@@ -294,8 +298,9 @@
             for d in near:
                 x_copy(s + 1, d).start()
         if s:
-            for d in range(1, ways):
-                mixed_copy(s - 1, d).start()
+            for c in range(cuts):
+                for d in range(1, ways):
+                    mixed_copy(s - 1, d, c).start()
         for d in far:
             project(s, d)
         for copy in stores[s]:
@@ -329,17 +334,21 @@
                 log_s[rows, :] = jnp.where(log_lane == h, top + jnp.log(total), log_s[rows, :])
             return carry
 
-        lax.fori_loop(0, heads, one_head, 0)
+        for c in range(cuts):
+            lax.fori_loop(c * heads // cuts, (c + 1) * heads // cuts, one_head, 0)
+            columns = slice(c * cut, (c + 1) * cut)
+            mixed_h[s, :, columns] = mixed_f[:, columns].astype(jnp.bfloat16)
+            if s == seqs - 1:
+                for d in range(1, ways):
+                    mixed_copy(s, d, c).start()
         log_ref[s] = jnp.transpose(log_s[...])[: log_ref.shape[1], :]
-        mixed_h[s] = mixed_f[...].astype(jnp.bfloat16)
         mixed_tok[s, :, own_columns] = mixed_h[s, span(me, shard), :]
-    for d in range(1, ways):
-        mixed_copy(seqs - 1, d).start()
 
     loads[4].wait()
     for s in range(seqs):
-        for d in range(1, ways):
-            mixed_copy(s, d).wait_recv()
+        for c in range(cuts):
+            for d in range(1, ways):
+                mixed_copy(s, d, c).wait_recv()
         rows = slice(s * shard, (s + 1) * shard)
         values = x_all[s, span(me, shard), :].astype(jnp.float32)
         values += mxu(mixed_tok[s], wo_v[...])
@@ -362,8 +371,9 @@
             x_copy(s, d).wait_send()
         for copy in x_relays(s):
             copy.wait_send()
-        for d in range(1, ways):
-            mixed_copy(s, d).wait_send()
+        for c in range(cuts):
+            for d in range(1, ways):
+                mixed_copy(s, d, c).wait_send()
         for copy in stores[s]:
             copy.wait()
     for copy in background + [own_cot] + last:
@@ -464,7 +474,16 @@
         )
         for group in range(groups)
     ]
-    cot_copy = send(cot_ref, arrived.at[1], f_send.at[groups], f_recv.at[groups], pair)
+    cot_copy = [
+        send(
+            cot_ref.at[i * groups : (i + 1) * groups],
+            arrived.at[1, i * groups : (i + 1) * groups],
+            f_send.at[groups + i],
+            f_recv.at[groups + i],
+            pair,
+        )
+        for i in range(2)
+    ]
     dn_copy = [
         send(
             dn_pair.at[chips[group]],
@@ -493,17 +512,18 @@
         copy.start()
     for copy in inward[1 : 2 * middle[0] - 1]:
         copy.start()
-    cot_copy.start()
+    for copy in cot_copy:
+        copy.start()
     own_rows.wait()
 
     def slab_of(half, group):
         return pl.ds(pl.multiple_of(half * rows + near[group] * (2 * slots), 2 * slots), 2 * slots)
 
-    def cot_half(half):
+    def cot_part(half, begin, end):
         def cot_step(i, carry):
             at = span(i, STEP)
-            cot = arrived[half].reshape(rows, width)
-            slope_v[half * rows : (half + 1) * rows, at] = mxu(
+            cot = arrived[half, begin:end].reshape((end - begin) * slots, width)
+            slope_v[half * rows + begin * slots : half * rows + end * slots, at] = mxu(
                 cot, down_v[at, :], ROWS_BY_ROWS
             ).astype(jnp.bfloat16)
             return carry
@@ -534,7 +554,6 @@
         shaped = total[...].reshape(2, slots, width)
         if half:
             dn_pair[chips[group]] = shaped.astype(jnp.bfloat16)
-            dn_copy[group].start()
         else:
             dn_own[chips[group]] = shaped
 
@@ -566,15 +585,32 @@
     def up_pair(group):
         forward[group].wait_recv()
         up_half(1, group)
+        if group not in early:
+            dn_copy[group].start()
+
+    def grad(target, left, right_ref, begin, end, block=0):
+        def grad_step(i, carry):
+            at = span(i, STEP)
+            right = right_ref[...].reshape(2 * rows, width)
+            out = mxu(left[:, at], right, COLS_BY_COLS).astype(jnp.bfloat16)
+            if block:
+                target[span(i, STEP // block)] = out.reshape(STEP // block, block, width)
+            else:
+                target[at, :] = out
+            return carry
+
+        lax.fori_loop(begin, end, grad_step, 0)
 
     pass_on(0)
     own_cot.wait()
     for copy in loads[: len(shards)]:
         copy.wait()
-    cot_half(0)
+    cot_part(0, 0, others)
     for copy in loads[len(shards) :]:
         copy.wait()
     up_half(0, 0)
+    cot_copy[0].wait_recv()
+    cot_part(1, 0, groups)
     for group in middle:
         pass_on(group)
         up_half(0, group)
@@ -584,50 +620,43 @@
         copy.start()
     for group in early[1:]:
         pass_on(group)
-    cot_copy.wait_recv()
-    cot_half(1)
+    cot_copy[1].wait_recv()
+    cot_part(1, groups, others)
     for group in early[1:]:
         up_half(0, group)
     for group in middle:
         up_pair(group)
-    up_pair(0)
+    for group in early:
+        up_pair(group)
+    for group in late:
+        pass_on(group)
+    dn_copy[0].start()
     for group in middle:
         finish(group)
-    for group in late:
-        pass_on(group)
-    for group in early[1:]:
-        up_pair(group)
     for group in late:
         up_half(0, group)
     for group in middle:
         out_half(1, group)
-    finish(0)
     for group in late:
         up_pair(group)
+    for group in early[1:]:
+        dn_copy[group].start()
+    for group in middle:
+        out_copy[group].start()
     for group in [*early, *late]:
         out_half(1, group)
-    for group in [*early[1:], *late]:
+    tokens_all = received.at[0 : 2 * others]
+    grad(up_v, slope_v, tokens_all, 0, 1)
+    for group in late:
         finish(group)
-    for copy in out_copy:
-        copy.start()
-
-    def grad(target, left, right_ref, block=0):
-        def grad_step(i, carry):
-            at = span(i, STEP)
-            right = right_ref[...].reshape(2 * rows, width)
-            out = mxu(left[:, at], right, COLS_BY_COLS).astype(jnp.bfloat16)
-            if block:
-                target[span(i, STEP // block)] = out.reshape(STEP // block, block, width)
-            else:
-                target[at, :] = out
-            return carry
-
-        lax.fori_loop(0, ff // STEP, grad_step, 0)
-
-    grad(up_v, slope_v, received.at[0 : 2 * others])
+    for group in [*early, *late]:
+        out_copy[group].start()
+    grad(up_v, slope_v, tokens_all, 1, ff // STEP)
+    for group in early:
+        finish(group)
     for copy in forward:
         copy.wait_send()
-    grad(received, hidden, arrived, slots)
+    grad(received, hidden, arrived, 0, ff // STEP, slots)
     first, every = size // slots, ff // slots
     stores = [
         pltpu.make_async_copy(source, target, o_sem.at[i])
@@ -646,7 +675,7 @@
         out_half(0, group)
     for copy in inward[: 2 * middle[0] - 1] + inward[2 * late[0] - 1 :]:
         copy.wait_send()
-    for copy in [cot_copy] + dn_copy + out_copy:
+    for copy in cot_copy + dn_copy + out_copy:
         copy.wait_send()
     for copy in outward + stores + [own_back]:
         copy.wait()
@@ -966,16 +995,25 @@
     scatter = []
     for j, (rest, land) in enumerate(((up_rest, up_land), (down_rest, down_land))):
         size = land.shape[1]
-        scatter += [
-            send(
-                rest.at[(i - 1) * size : i * size],
-                land.at[i - 1],
-                s_send.at[j, i],
-                s_recv.at[j, i],
-                {"sp": shards[i]},
-            )
-            for i in range(1, len(shards))
-        ]
+        first = size // 4
+        for part, (begin, end) in enumerate(((0, first), (first, size))):
+            scatter += [
+                send(
+                    rest.at[(i - 1) * size + begin : (i - 1) * size + end],
+                    land.at[i - 1, begin:end],
+                    s_send.at[j, part, i],
+                    s_recv.at[j, part, i],
+                    {"sp": shards[i]},
+                )
+                for i in range(1, len(shards))
+            ]
+    routed_back = exchange(others, result_ref, returned, c_send, c_recv)
+    pl.semaphore_wait(barrier, len(neighbours))
+    for copy in scatter[: len(shards) - 1]:
+        copy.start()
+    for copy in routed_back:
+        copy.start()
+
     small_own[...] = jnp.zeros_like(small_own)
     small_own[4:5, 0:LANES] = counts_ref[0:1, :]
     for s in range(seqs):
@@ -995,16 +1033,13 @@
         if s == 0:
             loads[4].wait()
         dmixed[s] = mxu(dattn[rows, :], wo_v[...], ROWS_BY_ROWS).astype(jnp.bfloat16)
-        if s == 0:
-            pl.semaphore_wait(barrier, len(neighbours))
         for d in range(1, ways):
             dmixed_copy(s, d).start()
-    for copy in scatter:
+    for copy in scatter[len(shards) - 1 :]:
         copy.start()
-    routed_back = exchange(others, result_ref, returned, c_send, c_recv)
     sum_o = Reduction(ways, columns, part_o, out_o, False, scratch[:15])
     sums_w = [
-        Reduction(ways, columns, parts_w.at[i], out, False, scratch[15 * (i + 1) : 15 * (i + 2)])
+        Reduction(ways, columns, parts_w.at[i], out, i == 0, scratch[15 * (i + 1) : 15 * (i + 2)])
         for i, out in enumerate((out_q, out_k, out_v))
     ]
     sum_q, sum_k, sum_v = sums_w
@@ -1072,11 +1107,34 @@
         if s == 0:
             for d in range(1, ways):
                 grad_copy(s, d).start()
-            for step in range(steps - 1):
-                sum_o.add_column(step)
-            for copy in routed_back[: 3 * others // 4 - 1]:
-                copy.start()
         grads_tok[s, :, span(me, 3 * width)] = grads_h[s, span(me, shard), :]
+
+    loads[9].wait()
+
+    def weight_step(i, carry):
+        at = span(i, BLOCK)
+        grad = mxu(normed_v[0, :, at], grads_h[0], COLS_BY_COLS)
+        for s in range(1, seqs):
+            grad += mxu(normed_v[s, :, at], grads_h[s], COLS_BY_COLS)
+        for j in range(3):
+            parts_w[j, at, :] = grad[:, j * width : (j + 1) * width].astype(jnp.bfloat16)
+        return carry
+
+    lax.fori_loop(0, model // BLOCK, weight_step, 0)
+    for total in (sum_v, sum_k, sum_q):
+        total.core_copy.start()
+
+    along, across = (sum_v, sum_k), (sum_q,)
+    for total in (*across, *along):
+        total.add_core()
+    for step in range(steps - 1):
+        sum_o.add_column(step)
+    for step in range(steps):
+        for total in (*across, *along):
+            piece = total.add_column(step)
+            if step == steps - 1:
+                total.piece[...] = piece.astype(jnp.bfloat16)
+                total.advance()
 
     o_land[0] = sum_o.add_column(steps - 1).astype(jnp.bfloat16)
     o_copy = [
@@ -1090,35 +1148,6 @@
         for d in range(1, ways)
     ]
     for copy in o_copy:
-        copy.start()
-
-    loads[9].wait()
-
-    def weight_step(i, carry):
-        at = span(i, BLOCK)
-        grad = mxu(normed_v[0, :, at], grads_h[0], COLS_BY_COLS)
-        for s in range(1, seqs):
-            grad += mxu(normed_v[s, :, at], grads_h[s], COLS_BY_COLS)
-        for j in range(3):
-            parts_w[j, at, :] = grad[:, j * width : (j + 1) * width].astype(jnp.bfloat16)
-        return carry
-
-    lax.fori_loop(0, model // BLOCK, weight_step, 0)
-    for total in (sum_v, sum_k, sum_q):
-        total.core_copy.start()
-
-    for total in (sum_v, sum_k, sum_q):
-        total.add_core()
-    for step in range(steps):
-        for total in (sum_v, sum_k, sum_q):
-            piece = total.add_column(step)
-            if step == steps - 1:
-                total.piece[...] = piece.astype(jnp.bfloat16)
-                total.advance()
-    for s in range(1, seqs):
-        for d in range(1, ways):
-            grad_copy(s, d).start()
-    for copy in routed_back[3 * others // 4 - 1 :]:
         copy.start()
 
     def norm_grad(s):
@@ -1142,22 +1171,28 @@
 
     for copy in loads[10:14]:
         copy.wait()
-    for _ in range(steps - 1):
-        for total in (sum_v, sum_k, sum_q):
-            total.advance()
-    for s in range(seqs - 1):
-        norm_grad(s)
-    for total in (sum_v, sum_k, sum_q):
+    for total in across:
         total.advance()
+    for s in range(1, seqs):
+        for d in range(1, ways):
+            grad_copy(s, d).start()
     total = o_land[0, :, span(me, width)].astype(jnp.float32)
     for d, copy in enumerate(o_copy):
         copy.wait()
         total += o_land[d + 1, :, 0:width].astype(jnp.float32)
     sum_o.piece[...] = total.astype(jnp.bfloat16)
     sum_o.advance()
+    for _ in range(steps - 1):
+        for total in along:
+            total.advance()
+    for total in across:
+        total.advance()
+    for _ in range(steps - 1):
+        sum_o.advance()
+    for s in range(seqs - 1):
+        norm_grad(s)
+    along[0].advance()
     norm_grad(seqs - 1)
-    for _ in range(steps):
-        sum_o.advance()
 
     stages = [[{"sp": peer[d]} for d in range(1, ways)], [{"dp": dp + 1 - 2 * core}]]
     stages.append([{"dp": 2 * lax.rem(dp // 2 + d, columns) + core} for d in range(1, columns)])
@@ -1177,14 +1212,17 @@
         for copy in copies:
             copy.start()
         if number == 0:
-            sum_v.advance()
-            sum_k.advance()
+            for total in (*along[1:], sum_o):
+                total.advance()
+            for _ in range(steps - 1):
+                for total in across:
+                    total.advance()
+            along[0].advance()
         elif number == 1:
-            sum_q.advance()
+            for total in along[1:]:
+                total.advance()
+        else:
             sum_o.advance()
-        else:
-            sum_v.advance()
-            sum_k.advance()
         total = source[...]
         for i, copy in enumerate(copies):
             copy.wait()
@@ -1203,8 +1241,8 @@
         rows = slice(s * shard, (s + 1) * shard)
         out = mxu(placer_v[:, rows], returned[...].reshape(-1, model), COLS_BY_COLS)
         block_ref[s] = (residual_v[rows, :] + out).astype(jnp.bfloat16)
-    sum_q.advance()
-    sum_o.advance()
+    for total in [*across, *along, sum_o]:
+        total.advance()
     for s in range(seqs):
         for d in range(1, ways):
             dmixed_copy(s, d).wait_send()
@@ -1371,8 +1409,8 @@
             pltpu.VMEM(flat, bf16),
             dma(seq_count, sp_ways),
             dma(seq_count, sp_ways),
-            dma(seq_count, sp_ways),
-            dma(seq_count, sp_ways),
+            dma(seq_count, 2, sp_ways),
+            dma(seq_count, 2, sp_ways),
             dma(dp_ways),
             dma(dp_ways),
             dma(5),
@@ -1432,10 +1470,10 @@
             dma(dp_ways),
             dma(dp_ways),
             dma(dp_ways),
-            dma(dp_ways // 2 + 1),
-            dma(dp_ways // 2 + 1),
-            dma(dp_ways // 2 + 1),
-            dma(dp_ways // 2 + 1),
+            dma(dp_ways // 2 + 2),
+            dma(dp_ways // 2 + 2),
+            dma(dp_ways // 2),
+            dma(dp_ways // 2),
             dma(dp_ways // 2),
             dma(dp_ways // 2),
         ],
@@ -1515,8 +1553,8 @@
             dma(seq_count, sp_ways),
             dma(dp_ways),
             dma(dp_ways),
-            dma(2, sp_ways // 2),
-            dma(2, sp_ways // 2),
+            dma(2, 2, sp_ways // 2),
+            dma(2, 2, sp_ways // 2),
             dma(sp_ways),
             dma(sp_ways),
             dma(small_slots),

time: 328 us -> 320 us (0.976)
  the two profiles are of different devices: /device:TPU:0 before, /device:TPU:9 now
where the time goes in v2:
time: 320 us; the launch traced here: 314 us
  Pallas kernels  313 us (98%)
    pallas_call x1, Pallas kernels, local(): pl.pallas_call(functools.partial(backward, sp_ways, dp_ways, head_dim), o...  135 us
    pallas_call x1, Pallas kernels, local(): pl.pallas_call(functools.partial(run_experts, dp_ways, sp_ways), out_shap...  102 us
    pallas_call x1, Pallas kernels, local(): pl.pallas_call(functools.partial(forward, sp_ways, dp_ways, head_dim), ou...  59.4 us
    pallas_call x1, Pallas kernels, local(): pl.pallas_call(functools.partial(finish, experts, row_count * dp_ways * s...  16.5 us

profile of v2, /device:TPU:9, one launch (start us, length us, event | category | flops | bytes accessed | tf_op | source)
XLA Modules:
  0.0 313.8 jit_solution(18219392372373470459)
XLA Ops:
  0.6 59.4 %shard_map.237 = (bf16[2,1024,1024]{2,1,0:T(8,128)(2,1)}, bf16[2,1024,256]{2,1,0:T(8,128)(2,1)}, bf16[2,1024,256]{2,1,0:T(8,128)(2,1)}, bf16[2,1024,256]{2,1,0:T...) custom-call(bf16[2,256,1024]{2,1,0:T(8,128)(2,1)} %x_ref.3, ...), custom_call_target="tpu_custom_call" | custom-call | tf_op jit(solution)/shard_map/pallas_call | solution.py:1374
  60.1 102.2 %shard_map.238 = (bf16[8,128,1024]{2,1,0:T(8,128)(2,1)}, bf16[8,128,1024]{2,1,0:T(8,128)(2,1)}, bf16[1024,1024]{1,0:T(8,128)(2,1)}, bf16[1024,1024]{1,0:T(8,128)...) custom-call(bf16[8,128,1024]{2,1,0:T(8,128)(2,1)} %get-tuple-element.52.outgoing_ref, ...), custom_call_target="tpu_custom_call" | custom-call | tf_op jit(solution)/shard_map/pallas_call | solution.py:1440
  162.2 134.5 %shard_map.239 = (bf16[1024,1024]{1,0:T(8,128)(2,1)}, bf16[1024,1024]{1,0:T(8,128)(2,1)}, bf16[1024,1024]{1,0:T(8,128)(2,1)}, bf16[1024,1024]{1,0:T(8,128)(2,1)}...) custom-call(bf16[8,128,1024]{2,1,0:T(8,128)(2,1)} %get-tuple-element, ...), custom_call_target="tpu_custom_call" | custom-call | tf_op jit(solution)/shard_map/pallas_call | solution.py:1507
  296.7 16.5 %shard_map.240 = (f32[1024,1024]{1,0:T(8,128)}, f32[1024,1024]{1,0:T(8,128)}, f32[1024,1024]{1,0:T(8,128)}, f32[1024,1024]{1,0:T(8,128)}, f32[1024,1024]{1,0:T(8...) custom-call(bf16[1024,1024]{1,0:T(8,128)(2,1)} %get-tuple-element.67, ...), custom_call_target="tpu_custom_call" | custom-call | tf_op jit(solution)/shard_map/pallas_call | solution.py:1598

commit v3 on v2

--- a/solution.py
+++ b/solution.py
@@ -128,8 +128,8 @@
     arrived_ref,
     placer_ref,
     residual_ref,
+    outgoing_ref,
     log_ref,
-    outgoing_ref,
     counts_ref,
     x_all,
     cot_v,
@@ -149,6 +149,7 @@
     log_s,
     residual_v,
     normed2,
+    outgoing_v,
     x_send,
     x_recv,
     m_send,
@@ -230,6 +231,10 @@
             {"sp": peer[d]},
         )
 
+    pl.semaphore_wait(barrier, len(neighbours))
+    for d in near:
+        x_copy(0, d).start()
+
     tokens = seqs * shard
     ids = ids_ref[...]
     named = lax.broadcasted_iota(jnp.int32, (LANES, tokens), 0) == ids
@@ -243,9 +248,6 @@
     placer_v[...] = jnp.where(places, 1.0, 0.0).astype(jnp.bfloat16)
     ones = jnp.ones((8, tokens), jnp.float32)
     counts_ref[...] = mxu(ones, named, ROWS_BY_ROWS)
-    pl.semaphore_wait(barrier, len(neighbours))
-    for d in near:
-        x_copy(0, d).start()
     loads[0].wait()
     cot_out[...] = (
         mxu(placer_v[...], cot_v[...]).astype(jnp.bfloat16).reshape(cot_out.shape)
@@ -290,13 +292,13 @@
             x_copy(s, d).wait_recv()
         for copy in x_relays(s):
             copy.start()
+        if s + 1 < seqs:
+            for d in near:
+                x_copy(s + 1, d).start()
         for d in near:
             project(s, d)
         for copy in x_relays(s):
             copy.wait_recv()
-        if s + 1 < seqs:
-            for d in near:
-                x_copy(s + 1, d).start()
         if s:
             for c in range(cuts):
                 for d in range(1, ways):
@@ -363,9 +365,20 @@
     ]
     for copy in last:
         copy.start()
-    outgoing_ref[...] = (
-        mxu(placer_v[...], normed2[...]).astype(jnp.bfloat16).reshape(outgoing_ref.shape)
-    )
+    for i in range(2):
+        part = slots * others // 2
+        rows = slice(i * part, (i + 1) * part)
+        blocks = pl.ds(i * others // 2, others // 2)
+        outgoing_v[blocks] = (
+            mxu(placer_v[rows, :], normed2[...])
+            .astype(jnp.bfloat16)
+            .reshape(others // 2, slots, model)
+        )
+        copy = pltpu.make_async_copy(
+            outgoing_v.at[blocks], outgoing_ref.at[blocks], store_sem.at[seqs + 1, i]
+        )
+        copy.start()
+        last.append(copy)
     for s in range(seqs):
         for d in near:
             x_copy(s, d).wait_send()
@@ -891,6 +904,8 @@
     block_ref,
     tokens_ref,
     small_out,
+    block_v,
+    tokens_v,
     back_v,
     placer_v,
     cot_v,
@@ -934,6 +949,7 @@
     small_send,
     small_recv,
     load_sem,
+    out_sem,
     *scratch,
 ):
     seqs, shard, model = x_v.shape
@@ -949,6 +965,11 @@
     neighbours += [{"dp": flip(dp, d)} for d in range(1, others)]
     for device in neighbours:
         pl.semaphore_signal(barrier, inc=1, device_id=device, device_id_type=MESH)
+    results = [
+        pltpu.make_async_copy(source.at[s], target.at[s], out_sem.at[i, s])
+        for i, (source, target) in enumerate(((tokens_v, tokens_ref), (block_v, block_ref)))
+        for s in range(seqs)
+    ]
     sources = (
         (back_ref, back_v),
         (placer_ref, placer_v),
@@ -1165,7 +1186,8 @@
         gain = gain1_ref[...]
         _, unit, rstd = norm_forward(x_v[s].astype(jnp.float32), gain, jnp.zeros_like(gain))
         dinput, gain_grad, shift_grad = norm_backward(dnormed, unit, rstd, gain)
-        tokens_ref[s] = (dresid[s] + dinput).astype(jnp.bfloat16)
+        tokens_v[s] = (dresid[s] + dinput).astype(jnp.bfloat16)
+        results[s].start()
         small_own[0:1, :] += gain_grad.reshape(1, model)
         small_own[1:2, :] += shift_grad.reshape(1, model)
 
@@ -1240,13 +1262,14 @@
     for s in range(seqs):
         rows = slice(s * shard, (s + 1) * shard)
         out = mxu(placer_v[:, rows], returned[...].reshape(-1, model), COLS_BY_COLS)
-        block_ref[s] = (residual_v[rows, :] + out).astype(jnp.bfloat16)
+        block_v[s] = (residual_v[rows, :] + out).astype(jnp.bfloat16)
+        results[seqs + s].start()
     for total in [*across, *along, sum_o]:
         total.advance()
     for s in range(seqs):
         for d in range(1, ways):
             dmixed_copy(s, d).wait_send()
-    for copy in scatter:
+    for copy in scatter + results:
         copy.wait()
     for total in [sum_o] + sums_w:
         total.finish()
@@ -1368,8 +1391,8 @@
         arrived,
         placer,
         residual_stream,
+        outgoing,
         log_total,
-        outgoing,
         counts,
     ) = pl.pallas_call(
         functools.partial(forward, sp_ways, dp_ways, head_dim),
@@ -1382,12 +1405,12 @@
             routed,
             shape(*slots),
             shape(*flat, dtype=f32),
+            routed,
             shape(seq_count, 8, seq_len, dtype=f32),
-            routed,
             shape(8, LANES, dtype=f32),
         ],
         in_specs=hbm * 6 + vmem(5),
-        out_specs=hbm * 8 + vmem(3),
+        out_specs=hbm * 9 + vmem(2),
         scratch_shapes=[
             whole_tokens,
             pltpu.VMEM(flat, bf16),
@@ -1407,6 +1430,7 @@
             pltpu.VMEM((seq_len, LANES), f32),
             pltpu.VMEM(flat, f32),
             pltpu.VMEM(flat, bf16),
+            pltpu.VMEM(routed.shape, bf16),
             dma(seq_count, sp_ways),
             dma(seq_count, sp_ways),
             dma(seq_count, 2, sp_ways),
@@ -1415,7 +1439,7 @@
             dma(dp_ways),
             dma(5),
             dma(seq_count),
-            dma(seq_count + 1, 4),
+            dma(seq_count + 2, 4),
             pltpu.SemaphoreType.DMA,
         ],
         compiler_params=params(0),
@@ -1515,8 +1539,10 @@
             shape(8, model_width, dtype=f32),
         ],
         in_specs=hbm * 17 + vmem(4),
-        out_specs=hbm * 6 + vmem(3),
+        out_specs=hbm * 8 + vmem(1),
         scratch_shapes=[
+            tokens,
+            tokens,
             pltpu.VMEM(routed.shape, bf16),
             pltpu.VMEM(placer.shape, bf16),
             pltpu.VMEM(flat, bf16),
@@ -1560,6 +1586,7 @@
             dma(small_slots),
             dma(small_slots),
             dma(15),
+            dma(2, seq_count),
         ]
         + reduction(model_width)
         + reduction(width) * 3,

time: 320 us -> 318 us (level)
  no operation moved by 1% of the time
where the time goes in v3:
time: 318 us; the launch traced here: 312 us
  Pallas kernels  311 us (98%)
    pallas_call x1, Pallas kernels, local(): pl.pallas_call(functools.partial(backward, sp_ways, dp_ways, head_dim), o...  134 us
    pallas_call x1, Pallas kernels, local(): pl.pallas_call(functools.partial(run_experts, dp_ways, sp_ways), out_shap...  102 us
    pallas_call x1, Pallas kernels, local(): pl.pallas_call(functools.partial(forward, sp_ways, dp_ways, head_dim), ou...  58.3 us
    pallas_call x1, Pallas kernels, local(): pl.pallas_call(functools.partial(finish, experts, row_count * dp_ways * s...  16.5 us

profile of v3, /device:TPU:9, one launch (start us, length us, event | category | flops | bytes accessed | tf_op | source)
XLA Modules:
  0.0 312.2 jit_solution(1278625053165543430)
XLA Ops:
  0.6 58.3 %shard_map.237 = (bf16[2,1024,1024]{2,1,0:T(8,128)(2,1)}, bf16[2,1024,256]{2,1,0:T(8,128)(2,1)}, bf16[2,1024,256]{2,1,0:T(8,128)(2,1)}, bf16[2,1024,256]{2,1,0:T...) custom-call(bf16[2,256,1024]{2,1,0:T(8,128)(2,1)} %x_ref.3, ...), custom_call_target="tpu_custom_call" | custom-call | tf_op jit(solution)/shard_map/pallas_call | solution.py:1397
  58.9 102.0 %shard_map.238 = (bf16[8,128,1024]{2,1,0:T(8,128)(2,1)}, bf16[8,128,1024]{2,1,0:T(8,128)(2,1)}, bf16[1024,1024]{1,0:T(8,128)(2,1)}, bf16[1024,1024]{1,0:T(8,128)...) custom-call(bf16[8,128,1024]{2,1,0:T(8,128)(2,1)} %get-tuple-element.52.outgoing_ref, ...), custom_call_target="tpu_custom_call" | custom-call | tf_op jit(solution)/shard_map/pallas_call | solution.py:1464
  160.9 134.3 %shard_map.239 = (bf16[1024,1024]{1,0:T(8,128)(2,1)}, bf16[1024,1024]{1,0:T(8,128)(2,1)}, bf16[1024,1024]{1,0:T(8,128)(2,1)}, bf16[1024,1024]{1,0:T(8,128)(2,1)}...) custom-call(bf16[8,128,1024]{2,1,0:T(8,128)(2,1)} %get-tuple-element, ...), custom_call_target="tpu_custom_call" | custom-call | tf_op jit(solution)/shard_map/pallas_call | solution.py:1531
  295.2 16.5 %shard_map.240 = (f32[1024,1024]{1,0:T(8,128)}, f32[1024,1024]{1,0:T(8,128)}, f32[1024,1024]{1,0:T(8,128)}, f32[1024,1024]{1,0:T(8,128)}, f32[1024,1024]{1,0:T(8...) custom-call(bf16[1024,1024]{1,0:T(8,128)(2,1)} %get-tuple-element.67, ...), custom_call_target="tpu_custom_call" | custom-call | tf_op jit(solution)/shard_map/pallas_call | solution.py:1625

commit v4 on v3

--- a/solution.py
+++ b/solution.py
@@ -1193,10 +1193,12 @@
 
     for copy in loads[10:14]:
         copy.wait()
+    for s in range(1, seqs):
+        grad_copy(s, 1).start()
     for total in across:
         total.advance()
     for s in range(1, seqs):
-        for d in range(1, ways):
+        for d in range(2, ways):
             grad_copy(s, d).start()
     total = o_land[0, :, span(me, width)].astype(jnp.float32)
     for d, copy in enumerate(o_copy):

time: 318 us -> 317 us (level)
  no operation moved by 1% of the time
where the time goes in v4:
time: 317 us; the launch traced here: 311 us
  Pallas kernels  310 us (98%)
    pallas_call x1, Pallas kernels, local(): pl.pallas_call(functools.partial(backward, sp_ways, dp_ways, head_dim), o...  133 us
    pallas_call x1, Pallas kernels, local(): pl.pallas_call(functools.partial(run_experts, dp_ways, sp_ways), out_shap...  102 us
    pallas_call x1, Pallas kernels, local(): pl.pallas_call(functools.partial(forward, sp_ways, dp_ways, head_dim), ou...  58.3 us
    pallas_call x1, Pallas kernels, local(): pl.pallas_call(functools.partial(finish, experts, row_count * dp_ways * s...  16.5 us

profile of v4, /device:TPU:9, one launch (start us, length us, event | category | flops | bytes accessed | tf_op | source)
XLA Modules:
  0.0 311.3 jit_solution(18044907356365080139)
XLA Ops:
  0.6 58.3 %shard_map.237 = (bf16[2,1024,1024]{2,1,0:T(8,128)(2,1)}, bf16[2,1024,256]{2,1,0:T(8,128)(2,1)}, bf16[2,1024,256]{2,1,0:T(8,128)(2,1)}, bf16[2,1024,256]{2,1,0:T...) custom-call(bf16[2,256,1024]{2,1,0:T(8,128)(2,1)} %x_ref.3, ...), custom_call_target="tpu_custom_call" | custom-call | tf_op jit(solution)/shard_map/pallas_call | solution.py:1399
  58.9 102.0 %shard_map.238 = (bf16[8,128,1024]{2,1,0:T(8,128)(2,1)}, bf16[8,128,1024]{2,1,0:T(8,128)(2,1)}, bf16[1024,1024]{1,0:T(8,128)(2,1)}, bf16[1024,1024]{1,0:T(8,128)...) custom-call(bf16[8,128,1024]{2,1,0:T(8,128)(2,1)} %get-tuple-element.52.outgoing_ref, ...), custom_call_target="tpu_custom_call" | custom-call | tf_op jit(solution)/shard_map/pallas_call | solution.py:1466
  160.9 133.4 %shard_map.239 = (bf16[1024,1024]{1,0:T(8,128)(2,1)}, bf16[1024,1024]{1,0:T(8,128)(2,1)}, bf16[1024,1024]{1,0:T(8,128)(2,1)}, bf16[1024,1024]{1,0:T(8,128)(2,1)}...) custom-call(bf16[8,128,1024]{2,1,0:T(8,128)(2,1)} %get-tuple-element, ...), custom_call_target="tpu_custom_call" | custom-call | tf_op jit(solution)/shard_map/pallas_call | solution.py:1533
  294.3 16.5 %shard_map.240 = (f32[1024,1024]{1,0:T(8,128)}, f32[1024,1024]{1,0:T(8,128)}, f32[1024,1024]{1,0:T(8,128)}, f32[1024,1024]{1,0:T(8,128)}, f32[1024,1024]{1,0:T(8...) custom-call(bf16[1024,1024]{1,0:T(8,128)(2,1)} %get-tuple-element.67, ...), custom_call_target="tpu_custom_call" | custom-call | tf_op jit(solution)/shard_map/pallas_call | solution.py:1627
